TPU v7x, 32 devices: a whole 2x2x4 slice. The times are simulated.
32 devices in a mesh: groups: 2 (over y), feat: 4 (over z), dp: 2 (over x), sub: 2 (over core).
Axes of the slice: x: 2, y: 2, z: 4, core: 2. Of those that a mesh axis runs over, the one named last changes fastest.
Arguments:
- snapshots: bfloat16 [1024, 16384], P(('groups', 'feat', 'dp', 'sub')), parts along dimension 0, may hold values from -6 to 6
- upstream: bfloat16 [1024, 16384], P(('groups', 'feat', 'dp', 'sub')), parts along dimension 0, may hold values from -0.79296875 to 0.79296875
- weights: bfloat16 [2, 128, 8, 128, 128], P(None, ('feat', 'sub')), may hold values from -0.1875 to 0.1875
- block_lists: int32 [2, 128, 8], replicated, may hold values from 0 to 127, as said below
Outputs:
- lifted: bfloat16 [1024, 16384], P(('groups', 'feat', 'dp', 'sub')), parts along dimension 0
- grad_weights: float32 [4, 128, 8, 128, 128], P('groups', ('feat', 'sub'), None, 'dp'), parts along dimension 0
There are 2 independent parts, one for each index of `groups`. A program takes and returns all parts, laid end to end along the dimension named above; an argument that names none is the same for every part. Nothing has to cross between parts.
Inputs may be any that keep to these rules, and one draw needn't show every extreme that they name: For each layer l and block j, block_lists[l, j, 0] // 16 equals j // 16, and for each slot s from 1 to 7, block_lists[l, j, s] // 16 equals (j XOR 2^(s-1)) // 16.
All inputs are finite; a program needn't handle non-finite values.
Results may differ from a plain program's by a relative error of at most 0.005.
Values may be sent and summed in bfloat16 or wider, within the bound.
A program may use at most 192 MiB of HBM per device.

v0:
```python
import jax
import jax.numpy as jnp
from jax import lax
from jax.sharding import PartitionSpec as P


def swapped(block, axis, distance):
    count = lax.axis_size(axis)
    route = []
    for low in range(count):
        high = low | 1 << distance
        if high != low and high < count:
            route += [(low, high), (high, low)]
    return lax.ppermute(block, axis, route)


def one_hot(indices, classes):
    return (indices[..., None] == jnp.arange(classes, dtype=jnp.int32)).astype(jnp.float32)


def per_device(snapshots, upstream, weights, block_lists):
    per_dev = weights.shape[1]
    slot_count = weights.shape[2]
    width_blk = weights.shape[3]
    levels = lax.axis_size(("feat", "sub")).bit_length() - 1
    local_slots = slot_count - levels
    position = lax.axis_index(("feat", "sub"))
    act_rows, cotangent = (
        lax.all_to_all(snapshots, ("feat", "sub"), split_axis=1, concat_axis=0, tiled=True),
        lax.all_to_all(upstream, ("feat", "sub"), split_axis=1, concat_axis=0, tiled=True),
    )
    row_count = act_rows.shape[0]
    own_lists = lax.dynamic_slice_in_dim(block_lists, position * per_dev, per_dev, 1) % per_dev
    level_order = list(range(levels))

    def forward(flat_acts, layer_id):
        blocks = flat_acts.reshape(row_count, per_dev, width_blk)
        sources = [blocks] * local_slots + [blocks] * levels
        for level_id in level_order:
            partner = swapped(flat_acts, ("feat", "sub"), level_id)
            sources[local_slots + level_id] = partner.reshape(row_count, per_dev, width_blk)
        picked = jnp.stack(
            [
                jnp.take(sources[slot_id], own_lists[layer_id, :, slot_id], axis=1)
                for slot_id in range(slot_count)
            ],
            axis=2,
        )
        pre_acts = jnp.einsum(
            "rjsa,jsab->rjb", picked, weights[layer_id], preferred_element_type=jnp.float32
        )
        return (jnp.tanh(pre_acts), picked)

    tanh_one, picked_one = forward(act_rows, 0)
    hidden = tanh_one.astype(jnp.bfloat16).reshape(row_count, per_dev * width_blk)
    tanh_two, picked_two = forward(hidden, 1)
    lifted = tanh_two.astype(jnp.bfloat16).reshape(row_count, per_dev * width_blk)
    lifted_rows = lax.all_to_all(lifted, ("feat", "sub"), split_axis=0, concat_axis=1, tiled=True)
    upper = cotangent.reshape(row_count, per_dev, width_blk).astype(jnp.float32)
    grad_two = (upper * (1.0 - tanh_two * tanh_two)).astype(jnp.bfloat16)
    second_w = weights[1]
    local_terms = jnp.einsum(
        "rjb,jsab->rjsa", grad_two, second_w[:, :local_slots], preferred_element_type=jnp.float32
    )
    hidden_grad = jnp.einsum(
        "rjsa,jsk->rka",
        local_terms,
        one_hot(own_lists[1, :, :local_slots], per_dev),
        precision=lax.Precision.HIGHEST,
    )
    for level_id in level_order:
        slot_id = local_slots + level_id
        terms = jnp.einsum(
            "rjb,jab->rja", grad_two, second_w[:, slot_id], preferred_element_type=jnp.float32
        )
        spread = jnp.einsum(
            "rja,jk->rka",
            terms,
            one_hot(own_lists[1, :, slot_id], per_dev),
            precision=lax.Precision.HIGHEST,
        )
        hidden_grad = hidden_grad + swapped(
            spread.astype(jnp.bfloat16), ("feat", "sub"), level_id
        ).astype(spread.dtype)
    grad_one = (hidden_grad * (1.0 - tanh_one * tanh_one)).astype(jnp.bfloat16)
    first_g = jnp.einsum("rjsa,rjb->jsab", picked_one, grad_one, preferred_element_type=jnp.float32)
    second_g = jnp.einsum(
        "rjsa,rjb->jsab", picked_two, grad_two, preferred_element_type=jnp.float32
    )
    grad_weights = lax.psum_scatter(
        jnp.stack([first_g, second_g]), "dp", scatter_dimension=3, tiled=True
    )
    return (lifted_rows, grad_weights)


def solution(mesh):
    in_specs = (
        P(("groups", "feat", "dp", "sub"), None),
        P(("groups", "feat", "dp", "sub"), None),
        P(None, ("feat", "sub"), None, None, None),
        P(),
    )
    out_specs = (
        P(("groups", "feat", "dp", "sub"), None),
        P("groups", ("feat", "sub"), None, "dp", None),
    )
    return jax.shard_map(
        per_device, mesh=mesh, in_specs=in_specs, out_specs=out_specs, check_vma=False
    )
```

profile of v0, /device:TPU:0, one launch (start us, length us, event | category | flops | bytes accessed | tf_op | source)
XLA Modules:
  0.0 493.0 jit_solution(6515439346419068159)
XLA Ops:
  7.2 2.3 copy.155
  9.5 6.3 %all-to-all-start = ((bf16[32,8,2048]{2,0,1:T(8,128)(2,1)}), bf16[32,8,2048]{2,0,1:T(8,128)(2,1)}, u32[]{:S(2)}, u32[]{:S(2)}) async-start(bf16[32,8,2048]{2,0,1:T(8,128)(2,1)} %bitcast.292), calls=%async_computation | async-start | bytes 2097152 | tf_op jit(solution)/shard_map/all_to_all | solution.py:29
  15.8 2.3 copy.154
  18.9 23.6 %all-to-all-done = bf16[32,8,2048]{2,0,1:T(8,128)(2,1)} async-done(((bf16[32,8,2048]{2,0,1:T(8,128)(2,1)}), bf16[32,8,2048]{2,0,1:T(8,128)(2,1)}, u32[]{:S(2)}, u32[]{:S(2)}) %all-to-all-start) | async-done | bytes 1048608 | tf_op jit(solution)/shard_map/all_to_all | solution.py:29
  42.5 3.6 all-to-all-start.2
  46.3 4.7 copy_bitcast_fusion
  51.3 1.7 collective-permute-start.1
  53.0 2.4 collective-permute-start.2
  55.4 17.7 %all-to-all-done.2 = bf16[32,8,2048]{2,0,1:T(8,128)(2,1)S(1)} async-done(((bf16[32,8,2048]{2,0,1:T(8,128)(2,1)}), bf16[32,8,2048]{2,0,1:T(8,128)(2,1)S(1)}, u32[]{:S(2)}, u32[]{:S(2)}) %all-to-all-start.2) | async-done | bytes 1048608 | tf_op jit(solution)/shard_map/all_to_all | solution.py:30
  73.8 1.8 copy.89
  75.6 1.4 copy.130
  77.4 1.7 gather_fusion
  79.0 1.8 gather_fusion.1
  80.8 1.7 gather_fusion.2
  83.9 2.5 bitcast_dynamic-update-slice_fusion.15
  86.5 2.5 bitcast_dynamic-update-slice_fusion.14
  89.0 2.5 bitcast_dynamic-update-slice_fusion.13
  94.2 1.5 copy.76
  96.3 10.2 %collective-permute-done.1 = bf16[256,2048]{1,0:T(8,128)(2,1)} collective-permute-done((bf16[256,2048]{1,0:T(8,128)(2,1)}, bf16[256,2048]{1,0:T(8,128)(2,1)}, u32[]{:S(2)}, u32[]{:S(2)}) %collective-permute-start.1) | collective-permute-done | bytes 1048608 | tf_op jit(solution)/shard_map/ppermute | solution.py:14
  106.5 1.5 copy.78
  108.0 1.3 copy.79
  109.3 8.4 %collective-permute-done.2 = bf16[256,2048]{1,0:T(8,128)(2,1)} collective-permute-done((bf16[256,2048]{1,0:T(8,128)(2,1)}, bf16[256,2048]{1,0:T(8,128)(2,1)}, u32[]{:S(2)}, u32[]{:S(2)}) %collective-permute-start.2) | collective-permute-done | bytes 1048608 | tf_op jit(solution)/shard_map/ppermute | solution.py:14
  117.7 1.5 copy.80
  119.2 1.5 copy.81
  121.4 2.0 gather_fusion.6
  123.4 2.0 gather_fusion.7
  129.3 8.8 %fusion.21 = (bf16[16,256,128]{1,2,0:T(8,128)(2,1)S(1)}, f32[16,256,128,1]{1,2,3,0:T(8,128)}) fusion(bf16[256,16,8,128]{3,0,2,1:T(8,128)(2,1)} %bitcast_dynamic-update-slice_fusion.8, bf16[2,16,8,128,128]{4,3,2,1,0:T(8,128)(2,1)} %param.8), kind=kOutput, calls=%fused_computation.44 | convolution fusion | flops 1074266112 | bytes 15728640 | tf_op jit(solution)/shard_map/rjsa,jsab->rjb/dot_general | solution.py:49
  138.1 1.9 collective-permute-start.5
  139.9 1.6 gather_fusion.8
  141.5 1.7 gather_fusion.9
  143.2 1.7 gather_fusion.10
  146.1 1.5 bitcast_dynamic-update-slice_fusion.7
  147.7 1.6 bitcast_dynamic-update-slice_fusion.6
  149.3 1.6 bitcast_dynamic-update-slice_fusion.5
  151.7 3.2 copy-done.1
  154.9 1.8 gather_fusion.13
  156.7 28.1 %collective-permute-done.4 = bf16[256,2048]{0,1:T(8,128)(2,1)} collective-permute-done((bf16[256,2048]{0,1:T(8,128)(2,1)S(1)}, bf16[256,2048]{0,1:T(8,128)(2,1)}, u32[]{:S(2)}, u32[]{:S(2)}) %collective-permute-start.4) | collective-permute-done | bytes 1048608 | tf_op jit(solution)/shard_map/ppermute | solution.py:14
  184.9 1.8 gather_fusion.14
  187.2 1.8 gather_fusion.15
  189.0 1.4 bitcast_dynamic-update-slice_fusion.2
  190.4 1.4 bitcast_dynamic-update-slice_fusion.1
  191.8 1.4 bitcast_dynamic-update-slice_fusion
  193.2 8.1 %fusion.14 = (bf16[256,16,128]{0,2,1:T(8,128)(2,1)S(1)}, f32[16,256,128,1]{1,2,0,3:T(8,128)}) fusion(f32[256,16,128]{0,2,1:T(8,128)} %copy.89, bf16[256,16,8,128]{0,3,1,2:T(8,128)(2,1)} %bitcast_dynamic-update-slice_fusion, bf16[2,16,8,128,128]{4,3,2,1,0:T(8,128)(2,1)} %param.8), kind=kOutput, calls=%fused_computation.35 | convolution fusion | flops 1075838976 | bytes 17825792 | tf_op jit(solution)/shard_map/rjsa,jsab->rjb/dot_general | solution.py:49
  201.3 1.7 convolution_bitcast_fusion.2
  203.0 2.8 convolution_bitcast_fusion.3
  205.8 1.5 convolution_bitcast_fusion.4
  207.4 5.6 %convolution_bitcast_fusion = f32[256,16,5,128]{3,0,2,1:T(8,128)} fusion(bf16[256,16,128]{0,2,1:T(8,128)(2,1)S(1)} %get-tuple-element.70, bf16[16,8,128,128]{3,2,0,1:T(8,128)(2,1)S(1)} %copy-done), kind=kOutput, calls=%fused_computation.25 | convolution fusion | flops 671088640 | bytes 14155776 | tf_op jit(solution)/shard_map/rjb,jsab->rjsa/dot_general | solution.py:62
  213.0 3.5 fusion.15
  216.5 2.4 copy.102
  219.2 4.7 fusion.17
  224.0 2.4 copy.99
  226.4 2.2 collective-permute-start.7
  228.5 3.3 fusion.19
  231.9 2.4 copy.96
  234.3 15.5 %fusion.23 = f32[16,256,128]{2,0,1:T(8,128)} fusion(f32[256,16,5,128]{3,0,2,1:T(8,128)} %convolution_bitcast_fusion, s32[16,5]{0,1:T(8,128)S(1)} %slice_bitcast_fusion.6), kind=kOutput, calls=%fused_computation.49 | convolution fusion | flops 503317760 | bytes 12583232 | tf_op jit(solution)/shard_map/rjsa,jsk->rka/dot_general | solution.py:65
  249.8 1.9 copy.93
  251.7 9.0 %fusion.7 = f32[1,16,8,128,128]{4,3,2,1,0:T(8,128)} fusion(bf16[256,16,8,128]{0,3,1,2:T(8,128)(2,1)} %bitcast_dynamic-update-slice_fusion, bf16[256,16,128]{0,2,1:T(8,128)(2,1)S(1)} %get-tuple-element.70), kind=kOutput, calls=%fused_computation.26 | convolution fusion | flops 1073741824 | bytes 17825792 | tf_op jit(solution)/shard_map/rjsa,rjb->jsab/dot_general | solution.py:87
  260.7 6.0 %collective-permute-done.8 = bf16[256,16,128]{0,2,1:T(8,128)(2,1)} collective-permute-done((bf16[256,16,128]{0,2,1:T(8,128)(2,1)}, bf16[256,16,128]{0,2,1:T(8,128)(2,1)}, u32[]{:S(2)}, u32[]{:S(2)}) %collective-permute-start.8) | collective-permute-done | bytes 1048608 | tf_op jit(solution)/shard_map/ppermute | solution.py:14
  266.7 7.2 %collective-permute-done.7 = bf16[256,16,128]{0,2,1:T(8,128)(2,1)} collective-permute-done((bf16[256,16,128]{0,2,1:T(8,128)(2,1)}, bf16[256,16,128]{0,2,1:T(8,128)(2,1)}, u32[]{:S(2)}, u32[]{:S(2)}) %collective-permute-start.7) | collective-permute-done | bytes 1048608 | tf_op jit(solution)/shard_map/ppermute | solution.py:14
  273.9 11.1 %convolution_bitcast_fusion.1 = f32[1,16,8,128,128]{4,3,2,1,0:T(8,128)} fusion(bf16[256,16,8,128]{3,0,2,1:T(8,128)(2,1)} %bitcast_dynamic-update-slice_fusion.8, f32[16,256,128,1]{1,2,3,0:T(8,128)} %get-tuple-element.69, bf16[256,16,128]{0,2,1:T(8,128)(2,1)} %collective-permute-done.8, bf16[256,16,128]{0,2,1:T(8,128)(2,1)} %collective-permute-done.7, ...), kind=kOutput, calls=%fused_computation.27 | convolution fusion | flops 1078984704 | bytes 24117248 | tf_op jit(solution)/shard_map/rjsa,rjb->jsab/dot_general | solution.py:86
  285.0 11.7 %pad_maximum_fusion = f32[2,16,8,128,128]{4,3,2,1,0:T(8,128)} fusion(f32[1,16,8,128,128]{4,3,2,1,0:T(8,128)} %fusion.7, f32[1,16,8,128,128]{4,3,2,1,0:T(8,128)} %convolution_bitcast_fusion.1), kind=kLoop, calls=%fused_computation.16 | loop fusion | flops 4194304 | bytes 33554432 | tf_op jit(solution)/shard_map/stack | solution.py:91
  296.8 1.6 copy-done.2
  300.2 29.6 %all_to_all.51 = bf16[8,32,2048]{2,1,0:T(8,128)(2,1)S(1)} all-to-all(bf16[8,32,2048]{2,1,0:T(8,128)(2,1)S(1)} %all_to_all.42), channel_id=1, replica_groups=mesh['groups'=2,'feat'=4,'dp'=2,'sub'=2] {'feat','sub'}, dimensions={0} | all-to-all | bytes 2097152 | tf_op jit(solution)/shard_map/all_to_all | solution.py:58
  330.9 154.8 %reduce-scatter.2.cloned.1.call-done = f32[2,16,8,64,128]{4,3,2,1,0:T(8,128)} async-done(((f32[2,16,8,128,128]{4,3,2,1,0:T(8,128)}), f32[2,16,8,64,128]{4,3,2,1,0:T(8,128)}) %reduce-scatter.2.cloned.1.call-update) | async-done | bytes 8388624 | tf_op jit(solution)/shard_map/reduce_scatter | solution.py:90
  (49 shorter events, 17.3 us)
Async XLA Ops:
  9.5 33.0 %all-to-all-start = ((bf16[32,8,2048]{2,0,1:T(8,128)(2,1)}), bf16[32,8,2048]{2,0,1:T(8,128)(2,1)}, u32[]{:S(2)}, u32[]{:S(2)}) async-start(bf16[32,8,2048]{2,0,1:T(8,128)(2,1)} %bitcast.292), calls=%async_computation | async-start | bytes 2097152 | tf_op jit(solution)/shard_map/all_to_all | solution.py:29
  42.5 30.7 %all-to-all-start.2 = ((bf16[32,8,2048]{2,0,1:T(8,128)(2,1)}), bf16[32,8,2048]{2,0,1:T(8,128)(2,1)S(1)}, u32[]{:S(2)}, u32[]{:S(2)}) async-start(bf16[32,8,2048]{2,0,1:T(8,128)(2,1)} %bitcast.291), calls=%async_computation.2 | async-start | bytes 2097152 | tf_op jit(solution)/shard_map/all_to_all | solution.py:30
  46.1 439.6 %reduce-scatter.2.cloned.1.call-start = ((), (), s32[]{:S(2)}) async-start(), calls=%async_computation.4 | async-start | bytes 25165824 | tf_op jit(solution)/shard_map/reduce_scatter | solution.py:90
  51.0 43.2 %collective-permute-start = (bf16[256,2048]{1,0:T(8,128)(2,1)}, bf16[256,2048]{1,0:T(8,128)(2,1)}, u32[]{:S(2)}, u32[]{:S(2)}) collective-permute-start(bf16[256,2048]{1,0:T(8,128)(2,1)} %bitcast.18), channel_id=1, source_target_pairs={{0,1},{1,0},{4,5},{5,4},{8,9},{9,8},{12,13},{13,12},{2,3},{3,2},{6... | collective-permute-start | bytes 3145736 | tf_op jit(solution)/shard_map/ppermute | solution.py:14
  51.3 55.2 %collective-permute-start.1 = (bf16[256,2048]{1,0:T(8,128)(2,1)}, bf16[256,2048]{1,0:T(8,128)(2,1)}, u32[]{:S(2)}, u32[]{:S(2)}) collective-permute-start(bf16[256,2048]{1,0:T(8,128)(2,1)} %bitcast.18), channel_id=1, source_target_pairs={{0,4},{4,0},{1,5},{5,1},{8,12},{12,8},{9,13},{13,9},{2,6},{6,2},{3... | collective-permute-start | bytes 3145736 | tf_op jit(solution)/shard_map/ppermute | solution.py:14
  53.0 64.7 %collective-permute-start.2 = (bf16[256,2048]{1,0:T(8,128)(2,1)}, bf16[256,2048]{1,0:T(8,128)(2,1)}, u32[]{:S(2)}, u32[]{:S(2)}) collective-permute-start(bf16[256,2048]{1,0:T(8,128)(2,1)} %bitcast.18), channel_id=1, source_target_pairs={{0,8},{8,0},{1,9},{9,1},{4,12},{12,4},{5,13},{13,5},{2,10},{10,2},... | collective-permute-start | bytes 3145736 | tf_op jit(solution)/shard_map/ppermute | solution.py:14
  138.1 13.6 %collective-permute-start.3 = (bf16[256,2048]{0,1:T(8,128)(2,1)S(1)}, bf16[256,2048]{0,1:T(8,128)(2,1)}, u32[]{:S(2)}, u32[]{:S(2)}) collective-permute-start(bf16[256,2048]{0,1:T(8,128)(2,1)S(1)} %bitcast.293), channel_id=1, source_target_pairs={{0,1},{1,0},{4,5},{5,4},{8,9},{9,8},{12,13},{13,12},{2,3},{3,2},{6... | collective-permute-start | bytes 3145736 | tf_op jit(solution)/shard_map/ppermute | solution.py:14
  138.1 46.8 %collective-permute-start.4 = (bf16[256,2048]{0,1:T(8,128)(2,1)S(1)}, bf16[256,2048]{0,1:T(8,128)(2,1)}, u32[]{:S(2)}, u32[]{:S(2)}) collective-permute-start(bf16[256,2048]{0,1:T(8,128)(2,1)S(1)} %bitcast.294), channel_id=1, source_target_pairs={{0,4},{4,0},{1,5},{5,1},{8,12},{12,8},{9,13},{13,9},{2,6},{6,2},{3... | collective-permute-start | bytes 3145736 | tf_op jit(solution)/shard_map/ppermute | solution.py:14
  138.1 49.1 %collective-permute-start.5 = (bf16[256,2048]{0,1:T(8,128)(2,1)S(1)}, bf16[256,2048]{0,1:T(8,128)(2,1)}, u32[]{:S(2)}, u32[]{:S(2)}) collective-permute-start(bf16[256,2048]{0,1:T(8,128)(2,1)S(1)} %bitcast.295), channel_id=1, source_target_pairs={{0,8},{8,0},{1,9},{9,1},{4,12},{12,4},{5,13},{13,5},{2,10},{10,2},... | collective-permute-start | bytes 3145736 | tf_op jit(solution)/shard_map/ppermute | solution.py:14
  151.6 3.2 copy-start.1
  201.3 6.0 %copy-start = (bf16[16,8,128,128]{3,2,0,1:T(8,128)(2,1)S(1)}, bf16[16,8,128,128]{3,2,0,1:T(8,128)(2,1)}, u32[]{:S(2)}) copy-start(bf16[16,8,128,128]{3,2,0,1:T(8,128)(2,1)} %copy_bitcast_fusion) | copy-start | bytes 12582916
  218.9 47.8 %collective-permute-start.8 = (bf16[256,16,128]{0,2,1:T(8,128)(2,1)}, bf16[256,16,128]{0,2,1:T(8,128)(2,1)}, u32[]{:S(2)}, u32[]{:S(2)}) collective-permute-start(bf16[256,16,128]{0,2,1:T(8,128)(2,1)} %bitcast.310), channel_id=1, source_target_pairs={{0,8},{8,0},{1,9},{9,1},{4,12},{12,4},{5,13},{13,5},{2,10},{10,2},... | collective-permute-start | bytes 3145736 | tf_op jit(solution)/shard_map/ppermute | solution.py:14
  226.4 47.5 %collective-permute-start.7 = (bf16[256,16,128]{0,2,1:T(8,128)(2,1)}, bf16[256,16,128]{0,2,1:T(8,128)(2,1)}, u32[]{:S(2)}, u32[]{:S(2)}) collective-permute-start(bf16[256,16,128]{0,2,1:T(8,128)(2,1)} %bitcast.311), channel_id=1, source_target_pairs={{0,4},{4,0},{1,5},{5,1},{8,12},{12,8},{9,13},{13,9},{2,6},{6,2},{3... | collective-permute-start | bytes 3145736 | tf_op jit(solution)/shard_map/ppermute | solution.py:14
  234.3 39.7 %collective-permute-start.6 = (bf16[256,16,128]{0,2,1:T(8,128)(2,1)}, bf16[256,16,128]{0,2,1:T(8,128)(2,1)}, u32[]{:S(2)}, u32[]{:S(2)}) collective-permute-start(bf16[256,16,128]{0,2,1:T(8,128)(2,1)} %bitcast.264), channel_id=1, source_target_pairs={{0,1},{1,0},{4,5},{5,4},{8,9},{9,8},{12,13},{13,12},{2,3},{3,2},{6... | collective-permute-start | bytes 3145736 | tf_op jit(solution)/shard_map/ppermute | solution.py:14
  296.7 1.6 copy-start.2
Sparse Core Ops, SparseCore 0:
  296.9 188.7 reduce-scatter.1
where the time goes:
time: 499 us; the launch traced here: 493 us
  waiting for transfers between devices  257 us (52%)
  matrix products  75.7 us (15%)
  local copies, waits for them, and re-layouts  60.7 us (12%)
  other arithmetic  36.8 us (7%)
  blocking collectives  29.6 us (6%)
  starting transfers between devices  18.7 us (4%)
  between operations  14.9 us (3%)
    reduce_scatter x1, waiting for transfers between devices, per_device(): lax.psum_scatter(jnp.stack([first_g, second_g]), 'dp', scatter_dimension=...  155 us
    ppermute x9, waiting for transfers between devices, swapped(): return lax.ppermute(block, axis, route)  60.4 us
    all_to_all x1, blocking collectives, per_device(): lax.all_to_all(lifted, ('feat', 'sub'), split_axis=0, concat_axis=1, tile...  29.6 us
    all_to_all x1, waiting for transfers between devices, per_device(): lax.all_to_all(snapshots, ('feat', 'sub'), split_axis=1, concat_axis=0, t...  23.6 us
    gather x16, local copies, waits for them, and re-layouts, forward(): jnp.take(sources[slot_id], own_lists[layer_id, :, slot_id], axis=1)  23 us
    unnamed x14, other arithmetic  21 us
    all_to_all x1, waiting for transfers between devices, per_device(): lax.all_to_all(upstream, ('feat', 'sub'), split_axis=1, concat_axis=0, ti...  17.7 us
    dot_general x2, matrix products, forward(): jnp.einsum('rjsa,jsab->rjb', picked, weights[layer_id], preferred_element...  16.9 us
  transfers between devices with their start and end apart: 12, of which 9 were waited for; matrix products, arithmetic and copies ran while one was open for 18% of the time, Pallas kernels for 0%

commit v1 on v0

v1 whole, which is shorter than its diff:
```python
import functools

import jax
import jax.numpy as jnp
from jax import lax
from jax.experimental import pallas as pl
from jax.experimental.pallas import tpu as pltpu
from jax.sharding import PartitionSpec as P

POS = ("feat", "sub")
VMEM_BYTES = 48 << 20


def swapped(block, axis, distance):
    count = lax.axis_size(axis)
    route = []
    for low in range(count):
        high = low | 1 << distance
        if high != low and high < count:
            route += [(low, high), (high, low)]
    return lax.ppermute(block, axis, route)


def gather_blocks(lists_ref, layer, j, sources, picked, sizes):
    per_dev, slots, local, blk = sizes
    for s in range(slots):
        ref = sources[max(0, s - local + 1)]
        idx = lists_ref[(layer * per_dev + j) * slots + s]
        picked[:, s * blk : (s + 1) * blk] = ref[:, pl.ds(pl.multiple_of(idx * blk, blk), blk)]


def store_gradient(dp, me_dp, grads, own_ref, other_ref, slots, blk):
    part = blk // dp
    if dp == 2:
        blocks = grads.reshape(slots, 2, part, blk)
        low, high = blocks[:, 0], blocks[:, 1]
        first = me_dp == 0
        own_ref[...] = jnp.where(first, low, high)
        other_ref[...] = jnp.where(first, high, low).astype(jnp.bfloat16)
    else:
        own_ref[...] = grads.reshape(slots, blk, blk)


def forward_kernel(sizes, count, lists_ref, *refs):
    per_dev, slots, local, blk = sizes
    sources, (w_ref, tanh_ref, hidden_ref, picked) = refs[:count], refs[count:]
    j = pl.program_id(0)
    gather_blocks(lists_ref, 0, j, sources, picked, sizes)
    pre = jnp.dot(
        picked[...], w_ref[...].reshape(slots * blk, blk), preferred_element_type=jnp.float32
    )
    out = jnp.tanh(pre)
    tanh_ref[...] = out
    hidden_ref[...] = out.astype(jnp.bfloat16)


def middle_kernel(sizes, count, dp, lists_ref, dp_ref, *refs):
    per_dev, slots, local, blk = sizes
    sources, refs = refs[:count], refs[count:]
    up_ref, w_ref, lifted_ref, own_sum = refs[:4]
    sent, refs = refs[4 : 3 + count], refs[3 + count :]
    grad_own, other = refs[0], (refs[1] if dp == 2 else None)
    refs = refs[2:] if dp == 2 else refs[1:]
    picked, sums = refs[0], refs[1:]
    j = pl.program_id(0)

    @pl.when(j == 0)
    def _():
        for ref in (own_sum, *sums):
            ref[...] = jnp.zeros_like(ref)

    gather_blocks(lists_ref, 1, j, sources, picked, sizes)
    w = w_ref[...].reshape(slots * blk, blk)
    out = jnp.tanh(jnp.dot(picked[...], w, preferred_element_type=jnp.float32))
    lifted_ref[...] = out.astype(jnp.bfloat16)
    grad = (up_ref[...].astype(jnp.float32) * (1.0 - out * out)).astype(jnp.bfloat16)
    totals = (own_sum, *sums)
    for s in range(slots):
        term = lax.dot_general(
            grad, w_ref[s], (((1,), (1,)), ((), ())), preferred_element_type=jnp.float32
        )
        idx = lists_ref[(per_dev + j) * slots + s]
        where = pl.ds(pl.multiple_of(idx * blk, blk), blk)
        totals[max(0, s - local + 1)][:, where] += term
    grads = lax.dot_general(
        picked[...], grad, (((0,), (0,)), ((), ())), preferred_element_type=jnp.float32
    )
    store_gradient(dp, dp_ref[0], grads, grad_own, other, slots, blk)

    @pl.when(j == per_dev - 1)
    def _():
        for ref, total in zip(sent, sums):
            ref[...] = total[...].astype(jnp.bfloat16)


def last_kernel(sizes, count, dp, lists_ref, dp_ref, *refs):
    per_dev, slots, local, blk = sizes
    sources, refs = refs[:count], refs[count:]
    tanh_ref, own_sum = refs[:2]
    received, refs = refs[2 : 1 + count], refs[1 + count :]
    grad_own, other, picked = refs if dp == 2 else (refs[0], None, refs[1])
    j = pl.program_id(0)
    gather_blocks(lists_ref, 0, j, sources, picked, sizes)
    total = own_sum[...]
    for ref in received:
        total = total + ref[...].astype(jnp.float32)
    out = tanh_ref[...]
    grad = (total * (1.0 - out * out)).astype(jnp.bfloat16)
    grads = lax.dot_general(
        picked[...], grad, (((0,), (0,)), ((), ())), preferred_element_type=jnp.float32
    )
    store_gradient(dp, dp_ref[0], grads, grad_own, other, slots, blk)


def per_device(snapshots, upstream, weights, block_lists):
    _, per_dev, slots, blk, _ = weights.shape
    levels = lax.axis_size(POS).bit_length() - 1
    dp = lax.axis_size("dp")
    count = levels + 1
    local = slots - levels
    position = lax.axis_index(POS)
    lists = (
        lax.dynamic_slice_in_dim(block_lists, position * per_dev, per_dev, 1) % per_dev
    ).reshape(-1)
    me_dp = lax.axis_index("dp").astype(jnp.int32).reshape(1)
    acts = lax.all_to_all(snapshots, POS, split_axis=1, concat_axis=0, tiled=True)
    upper = lax.all_to_all(upstream, POS, split_axis=1, concat_axis=0, tiled=True)
    rows, width = acts.shape
    sizes = (per_dev, slots, local, blk)
    part = blk // dp
    params = pltpu.CompilerParams(vmem_limit_bytes=VMEM_BYTES)

    whole = pl.BlockSpec((rows, width), lambda j, *_: (0, 0))
    column = pl.BlockSpec((rows, blk), lambda j, *_: (0, j))
    picked_scratch = pltpu.VMEM((rows, slots * blk), jnp.bfloat16)

    def weight_spec(layer):
        return pl.BlockSpec((None, None, slots, blk, blk), lambda j, *_: (layer, j, 0, 0, 0))

    def array(shape, dtype):
        return jax.ShapeDtypeStruct(shape, dtype)

    def with_partners(flat):
        return (flat, *(swapped(flat, POS, level) for level in range(levels)))

    if dp == 2:
        grad_spec = pl.BlockSpec((None, slots, part, blk), lambda j, *_: (j, 0, 0, 0))
        grad_specs = [grad_spec, grad_spec]
        grad_shapes = [
            array((per_dev, slots, part, blk), jnp.float32),
            array((per_dev, slots, part, blk), jnp.bfloat16),
        ]
    else:
        grad_specs = [pl.BlockSpec((None, slots, blk, blk), lambda j, *_: (j, 0, 0, 0))]
        grad_shapes = [array((per_dev, slots, blk, blk), jnp.float32)]

    def cost(products, read):
        flops = products * 2 * rows * per_dev * slots * blk * blk
        return pl.CostEstimate(flops=flops, bytes_accessed=read, transcendentals=rows * width)

    act_sources = with_partners(acts)
    tanh_one, hidden = pl.pallas_call(
        functools.partial(forward_kernel, sizes, count),
        grid_spec=pltpu.PrefetchScalarGridSpec(
            num_scalar_prefetch=1,
            grid=(per_dev,),
            in_specs=[whole] * count + [weight_spec(0)],
            out_specs=[column, column],
            scratch_shapes=[picked_scratch],
        ),
        out_shape=[array((rows, width), jnp.float32), array((rows, width), jnp.bfloat16)],
        compiler_params=params,
        cost_estimate=cost(1, 12 << 20),
        name="layer_one",
    )(lists, *act_sources, weights)

    hidden_sources = with_partners(hidden)
    middle = pl.pallas_call(
        functools.partial(middle_kernel, sizes, count, dp),
        grid_spec=pltpu.PrefetchScalarGridSpec(
            num_scalar_prefetch=2,
            grid=(per_dev,),
            in_specs=[whole] * count + [column, weight_spec(1)],
            out_specs=[column] + [whole] * count + grad_specs,
            scratch_shapes=[picked_scratch] + [pltpu.VMEM((rows, width), jnp.float32)] * levels,
        ),
        out_shape=[array((rows, width), jnp.bfloat16), array((rows, width), jnp.float32)]
        + [array((rows, width), jnp.bfloat16)] * levels
        + grad_shapes,
        compiler_params=params,
        cost_estimate=cost(3, 32 << 20),
        name="layer_two",
    )(lists, me_dp, *hidden_sources, upper, weights)
    lifted, own_sum, sent, second = middle[0], middle[1], middle[2 : 2 + levels], middle[2 + levels :]
    lifted_rows = lax.all_to_all(lifted, POS, split_axis=0, concat_axis=1, tiled=True)
    received = [swapped(block, POS, level) for level, block in enumerate(sent)]

    first = pl.pallas_call(
        functools.partial(last_kernel, sizes, count, dp),
        grid_spec=pltpu.PrefetchScalarGridSpec(
            num_scalar_prefetch=2,
            grid=(per_dev,),
            in_specs=[whole] * count + [column] * (count + 1),
            out_specs=grad_specs,
            scratch_shapes=[picked_scratch],
        ),
        out_shape=grad_shapes,
        compiler_params=params,
        cost_estimate=cost(1, 24 << 20),
        name="layer_one_gradient",
    )(lists, me_dp, *act_sources, tanh_one, own_sum, *received)

    if dp == 2:
        grad_weights = jnp.stack(
            [
                own + swapped(other, "dp", 0).astype(jnp.float32)
                for own, other in (first, second)
            ]
        )
    else:
        grad_weights = lax.psum_scatter(
            jnp.stack([first[0], second[0]]), "dp", scatter_dimension=3, tiled=True
        )
    return (lifted_rows, grad_weights)


def solution(mesh):
    in_specs = (
        P(("groups", "feat", "dp", "sub"), None),
        P(("groups", "feat", "dp", "sub"), None),
        P(None, ("feat", "sub"), None, None, None),
        P(),
    )
    out_specs = (
        P(("groups", "feat", "dp", "sub"), None),
        P("groups", ("feat", "sub"), None, "dp", None),
    )
    return jax.shard_map(
        per_device, mesh=mesh, in_specs=in_specs, out_specs=out_specs, check_vma=False
    )
```

time: 499 us -> 294 us (0.59)
  waiting for transfers between devices: 257 us -> 174 us
  matrix products: 75.7 us -> 0 us
  local copies, waits for them, and re-layouts: 60.7 us -> 5.89 us
  Pallas kernels: 0 us -> 51.2 us
  other arithmetic: 36.8 us -> 8.76 us
  between operations: 14.9 us -> 0.74 us
    reduce_scatter x1 -> x0, waiting for transfers between devices: 155 us -> none  [per_device(): lax.psum_scatter(jnp.stack([first_g, second_g]), 'dp', scatter_dimension=...]
    ppermute x9 -> x11, waiting for transfers between devices: 60.4 us -> 167 us  [swapped(): return lax.ppermute(block, axis, route)]
    dot_general x12 -> x0, matrix products: 75.7 us -> none  [the longest x2 16.9 us: forward(): jnp.einsum('rjsa,jsab->rjb', picked, weights[layer_id], preferred_element...]
    pallas_call x0 -> x3, Pallas kernels: none -> 51.2 us  [the longest x1 22 us: per_device(): pl.pallas_call(functools.partial(middle_kernel, sizes, count, dp), grid_s...]
    all_to_all x2, waiting for transfers between devices: 41.3 us -> 6.59 us  [the longest x1 3.36 us: per_device(): lax.all_to_all(lifted, POS, split_axis=0, concat_axis=1, tiled=True)]
    gather x16 -> x0, local copies, waits for them, and re-layouts: 23 us -> none  [forward(): jnp.take(sources[slot_id], own_lists[layer_id, :, slot_id], axis=1)]
    unnamed x14 -> x0, other arithmetic: 21 us -> none
    dot_general x4 -> x0, local copies, waits for them, and re-layouts: 9.19 us -> none  [the longest x3 7.26 us: per_device(): jnp.einsum('rja,jk->rka', terms, one_hot(own_lists[1, :, slot_id], per_de...]
  transfers between devices with their start and end apart: 12 -> 13, of which waited for: 9 -> 9; matrix products, arithmetic and copies ran while one was open for 18% -> 2% of each run, Pallas kernels for 0% -> 10%
where the time goes in v1:
time: 294 us; the launch traced here: 293 us
  waiting for transfers between devices  174 us (59%)
  Pallas kernels  51.2 us (17%)
  blocking collectives  32.7 us (11%)
  starting transfers between devices  19.7 us (7%)
  other arithmetic  8.76 us (3%)
  local copies, waits for them, and re-layouts  5.89 us (2%)
    ppermute x11, waiting for transfers between devices, swapped(): return lax.ppermute(block, axis, route)  167 us
    all_to_all x1, blocking collectives, per_device(): lax.all_to_all(snapshots, POS, split_axis=1, concat_axis=0, tiled=True)  32.7 us
    pallas_call x1, Pallas kernels, per_device(): pl.pallas_call(functools.partial(middle_kernel, sizes, count, dp), grid_s...  22 us
    pallas_call x1, Pallas kernels, per_device(): pl.pallas_call(functools.partial(last_kernel, sizes, count, dp), grid_spe...  15.7 us
    pallas_call x1, Pallas kernels, per_device(): pl.pallas_call(functools.partial(forward_kernel, sizes, count), grid_spec...  13.5 us
    ppermute x11, starting transfers between devices, swapped(): return lax.ppermute(block, axis, route)  11.2 us
    another operation x3, other arithmetic, per_device(): jnp.stack([own + swapped(other, 'dp', 0).astype(jnp.float32) for own, oth...  8.68 us
  transfers between devices with their start and end apart: 13, of which 9 were waited for; matrix products, arithmetic and copies ran while one was open for 2% of the time, Pallas kernels for 10%

profile of v1, /device:TPU:0, one launch (start us, length us, event | category | flops | bytes accessed | tf_op | source)
XLA Modules:
  0.0 292.6 jit_solution(16946374545196652183)
XLA Ops:
  0.6 0.0 copy-start.2
  0.6 0.0 copy-start.3
  0.6 1.4 copy.19
  2.1 32.7 %all_to_all.57 = bf16[32,8,2048]{2,0,1:T(8,128)(2,1)S(1)} all-to-all(bf16[32,8,2048]{2,0,1:T(8,128)(2,1)S(1)} %bitcast.30), channel_id=1, replica_groups=mesh['groups'=2,'feat'=4,'dp'=2,'sub'=2] {'feat','sub'}, dimensions={1} | all-to-all | bytes 2097152 | tf_op jit(solution)/shard_map/all_to_all | solution.py:126
  34.8 0.0 collective-permute-start
  34.8 0.0 collective-permute-start.1
  34.8 1.9 collective-permute-start.2
  36.7 0.0 copy-done.2
  36.7 1.0 copy.18
  37.7 4.2 %all-to-all-start.1 = ((bf16[32,8,2048]{2,0,1:T(8,128)(2,1)}), bf16[32,8,2048]{2,0,1:T(8,128)(2,1)}, u32[]{:S(2)}, u32[]{:S(2)}) async-start(bf16[32,8,2048]{2,0,1:T(8,128)(2,1)} %bitcast.29), calls=%async_computation.1 | async-start | bytes 2097152 | tf_op jit(solution)/shard_map/all_to_all | solution.py:127
  42.0 0.0 copy-done.3
  42.0 0.1 add_select_fusion
  42.1 0.1 copy.9
  42.1 0.1 reshape.19.lists_ref
  42.2 0.0 collective-permute-done.refs_1_
  42.2 39.6 %collective-permute-done.1.refs_2_ = bf16[256,2048]{1,0:T(8,128)(2,1)S(1)} collective-permute-done((bf16[256,2048]{1,0:T(8,128)(2,1)S(1)}, bf16[256,2048]{1,0:T(8,128)(2,1)S(1)}, u32[]{:S(2)}, u32[]{:S(2)}) %collective-permute-start.1) | collective-permute-done | bytes 1048608 | tf_op jit(solution)/shard_map/ppermute | solution.py:21
  81.9 4.0 %collective-permute-done.2.refs_3_ = bf16[256,2048]{1,0:T(8,128)(2,1)} collective-permute-done((bf16[256,2048]{1,0:T(8,128)(2,1)S(1)}, bf16[256,2048]{1,0:T(8,128)(2,1)}, u32[]{:S(2)}, u32[]{:S(2)}) %collective-permute-start.2) | collective-permute-done | bytes 1048608 | tf_op jit(solution)/shard_map/ppermute | solution.py:21
  85.9 13.5 %layer_one.1 = (f32[256,2048]{1,0:T(8,128)}, bf16[256,2048]{1,0:T(8,128)(2,1)}) custom-call(s32[256]{0:T(256)S(1)} %reshape.19.lists_ref, bf16[256,2048]{1,0:T(8,128)(2,1)S(1)} %bitcast.26, bf16[256,2048]{1,0:T(8,128)(2,1)S(1)} %collective-permute-done.refs_1_, bf16[256,2048]{1,0:T(8,128)(2,1)S(1)} %collective-permute-done.1.refs_2_, ...), custom_call_target="tpu_custom_call" | custom-call | flops 1073741824 | bytes 12582912 | tf_op jit(solution)/shard_map/layer_one/pallas_call | solution.py:162
  99.4 0.0 collective-permute-start.3
  99.4 0.0 collective-permute-start.4
  99.5 4.1 %collective-permute-start.5 = (bf16[256,2048]{1,0:T(8,128)(2,1)}, bf16[256,2048]{1,0:T(8,128)(2,1)}, u32[]{:S(2)}, u32[]{:S(2)}) collective-permute-start(bf16[256,2048]{1,0:T(8,128)(2,1)} %get-tuple-element.13.refs_0_), channel_id=1, source_target_pairs={{0,8},{8,0},{1,9},{9,1},{4,12},{12,4},{5,13},{13,5},{2,10},{10,2},... | collective-permute-start | bytes 3145736 | tf_op jit(solution)/shard_map/ppermute | solution.py:21
  103.6 3.2 %all-to-all-done.1 = bf16[32,8,2048]{2,0,1:T(8,128)(2,1)} async-done(((bf16[32,8,2048]{2,0,1:T(8,128)(2,1)}), bf16[32,8,2048]{2,0,1:T(8,128)(2,1)}, u32[]{:S(2)}, u32[]{:S(2)}) %all-to-all-start.1) | async-done | bytes 1048608 | tf_op jit(solution)/shard_map/all_to_all | solution.py:127
  106.8 0.0 collective-permute-done.3.refs_1_
  106.8 42.7 %collective-permute-done.4.refs_2_ = bf16[256,2048]{1,0:T(8,128)(2,1)} collective-permute-done((bf16[256,2048]{1,0:T(8,128)(2,1)}, bf16[256,2048]{1,0:T(8,128)(2,1)}, u32[]{:S(2)}, u32[]{:S(2)}) %collective-permute-start.4) | collective-permute-done | bytes 1048608 | tf_op jit(solution)/shard_map/ppermute | solution.py:21
  149.6 1.8 collective-permute-done.5.refs_3_
  151.3 22.0 %layer_two.1 = (bf16[256,2048]{1,0:T(8,128)(2,1)S(1)}, f32[256,2048]{1,0:T(8,128)}, bf16[256,2048]{1,0:T(8,128)(2,1)}, bf16[256,2048]{1,0:T(8,128)(2,1)}, bf16[2...) custom-call(s32[256]{0:T(256)S(1)} %reshape.19.lists_ref, s32[1]{0:T(128)} %bitcast.dp_ref, ...), custom_call_target="tpu_custom_call" | custom-call | flops 3221225472 | bytes 33554432 | tf_op jit(solution)/shard_map/layer_two/pallas_call | solution.py:178
  173.3 0.0 copy-start
  173.3 1.0 copy-done
  174.3 0.0 collective-permute-start.6
  174.3 0.0 collective-permute-start.7
  174.3 2.1 collective-permute-start.8
  176.4 1.5 collective-permute-start.10
  177.9 4.2 %all-to-all-start.2 = ((bf16[8,32,2048]{2,1,0:T(8,128)(2,1)}), bf16[8,32,2048]{2,1,0:T(8,128)(2,1)}, u32[]{:S(2)}, u32[]{:S(2)}) async-start(bf16[8,32,2048]{2,1,0:T(8,128)(2,1)} %bitcast.28), calls=%async_computation.2 | async-start | bytes 2097152 | tf_op jit(solution)/shard_map/all_to_all | solution.py:195
  182.1 0.0 collective-permute-done.6.refs_6_
  182.1 39.8 %collective-permute-done.7.refs_7_ = bf16[256,2048]{1,0:T(8,128)(2,1)} collective-permute-done((bf16[256,2048]{1,0:T(8,128)(2,1)}, bf16[256,2048]{1,0:T(8,128)(2,1)}, u32[]{:S(2)}, u32[]{:S(2)}) %collective-permute-start.7) | collective-permute-done | bytes 1048608 | tf_op jit(solution)/shard_map/ppermute | solution.py:21
  222.0 3.5 %collective-permute-done.8.refs_8_ = bf16[256,2048]{1,0:T(8,128)(2,1)} collective-permute-done((bf16[256,2048]{1,0:T(8,128)(2,1)}, bf16[256,2048]{1,0:T(8,128)(2,1)}, u32[]{:S(2)}, u32[]{:S(2)}) %collective-permute-start.8) | collective-permute-done | bytes 1048608 | tf_op jit(solution)/shard_map/ppermute | solution.py:21
  225.5 15.7 %layer_one_gradient.1 = (f32[16,8,64,128]{3,2,1,0:T(8,128)}, bf16[16,8,64,128]{3,2,1,0:T(8,128)(2,1)}) custom-call(s32[256]{0:T(256)S(1)} %reshape.19.lists_ref, s32[1]{0:T(128)} %bitcast.dp_ref, bf16[256,2048]{1,0:T(8,128)(2,1)S(1)} %bitcast.27, bf16[256,2048]{1,0:T(8,128)(2,1)S(1)} %collective-permute-done.refs_1_, ...), custom_call_target="tpu_custom_call" | custom-call | flops 1073741824 | bytes 25165824 | tf_op jit(solution)/shard_map/layer_one_gradient/pallas_call | solution.py:198
  241.2 1.5 collective-permute-start.9
  242.7 3.4 %all-to-all-done.2 = bf16[8,32,2048]{2,1,0:T(8,128)(2,1)} async-done(((bf16[8,32,2048]{2,1,0:T(8,128)(2,1)}), bf16[8,32,2048]{2,1,0:T(8,128)(2,1)}, u32[]{:S(2)}, u32[]{:S(2)}) %all-to-all-start.2) | async-done | bytes 1048608 | tf_op jit(solution)/shard_map/all_to_all | solution.py:195
  246.1 2.3 copy.15
  248.4 0.0 collective-permute-done.10
  248.4 0.0 copy-start.1
  248.4 3.7 %add_bitcast_fusion = f32[1,16,8,64,128]{4,3,2,1,0:T(8,128)S(1)} fusion(f32[16,8,64,128]{3,2,1,0:T(8,128)} %get-tuple-element.22, bf16[16,8,64,128]{3,2,1,0:T(8,128)(2,1)} %collective-permute-done.10), kind=kLoop, calls=%fused_computation.1 | loop fusion | flops 2097152 | bytes 10485760 | tf_op jit(solution)/shard_map/stack | solution.py:214
  252.1 35.5 %collective-permute-done.9 = bf16[16,8,64,128]{3,2,1,0:T(8,128)(2,1)S(1)} collective-permute-done((bf16[16,8,64,128]{3,2,1,0:T(8,128)(2,1)}, bf16[16,8,64,128]{3,2,1,0:T(8,128)(2,1)S(1)}, u32[]{:S(2)}, u32[]{:S(2)}) %collective-permute-start.9) | collective-permute-done | bytes 2097184 | tf_op jit(solution)/shard_map/ppermute | solution.py:21
  287.6 0.0 copy-done.1
  287.6 0.7 add_bitcast_fusion.1
  288.3 4.2 %pad_maximum_fusion = f32[2,16,8,64,128]{4,3,2,1,0:T(8,128)} fusion(f32[1,16,8,64,128]{4,3,2,1,0:T(8,128)S(1)} %add_bitcast_fusion, f32[1,16,8,64,128]{4,3,2,1,0:T(8,128)S(1)} %add_bitcast_fusion.1), kind=kLoop, calls=%fused_computation | loop fusion | flops 2097152 | bytes 16777216 | tf_op jit(solution)/shard_map/stack | solution.py:214
Async XLA Ops:
  0.6 36.0 %copy-start.2 = (bf16[32,16384]{1,0:T(8,128)(2,1)S(1)}, bf16[32,16384]{1,0:T(8,128)(2,1)}, u32[]{:S(2)}) copy-start(bf16[32,16384]{1,0:T(8,128)(2,1)} %param.5) | copy-start | bytes 3145732
  0.6 41.3 %copy-start.3 = (s32[2,128,8]{1,2,0:T(8,128)S(1)}, s32[2,128,8]{1,2,0:T(8,128)}, u32[]{:S(2)}) copy-start(s32[2,128,8]{1,2,0:T(8,128)} %param.7) | copy-start | bytes 24580
  34.8 7.5 %collective-permute-start = (bf16[256,2048]{1,0:T(8,128)(2,1)S(1)}, bf16[256,2048]{1,0:T(8,128)(2,1)S(1)}, u32[]{:S(2)}, u32[]{:S(2)}) collective-permute-start(bf16[256,2048]{1,0:T(8,128)(2,1)S(1)} %bitcast.23), channel_id=1, source_target_pairs={{0,1},{1,0},{4,5},{5,4},{8,9},{9,8},{12,13},{13,12},{2,3},{3,2},{6... | collective-permute-start | bytes 3145736 | tf_op jit(solution)/shard_map/ppermute | solution.py:21
  34.8 47.1 %collective-permute-start.1 = (bf16[256,2048]{1,0:T(8,128)(2,1)S(1)}, bf16[256,2048]{1,0:T(8,128)(2,1)S(1)}, u32[]{:S(2)}, u32[]{:S(2)}) collective-permute-start(bf16[256,2048]{1,0:T(8,128)(2,1)S(1)} %bitcast.24), channel_id=1, source_target_pairs={{0,4},{4,0},{1,5},{5,1},{8,12},{12,8},{9,13},{13,9},{2,6},{6,2},{3... | collective-permute-start | bytes 3145736 | tf_op jit(solution)/shard_map/ppermute | solution.py:21
  34.8 51.1 %collective-permute-start.2 = (bf16[256,2048]{1,0:T(8,128)(2,1)S(1)}, bf16[256,2048]{1,0:T(8,128)(2,1)}, u32[]{:S(2)}, u32[]{:S(2)}) collective-permute-start(bf16[256,2048]{1,0:T(8,128)(2,1)S(1)} %bitcast.25), channel_id=1, source_target_pairs={{0,8},{8,0},{1,9},{9,1},{4,12},{12,4},{5,13},{13,5},{2,10},{10,2},... | collective-permute-start | bytes 3145736 | tf_op jit(solution)/shard_map/ppermute | solution.py:21
  37.7 69.1 %all-to-all-start.1 = ((bf16[32,8,2048]{2,0,1:T(8,128)(2,1)}), bf16[32,8,2048]{2,0,1:T(8,128)(2,1)}, u32[]{:S(2)}, u32[]{:S(2)}) async-start(bf16[32,8,2048]{2,0,1:T(8,128)(2,1)} %bitcast.29), calls=%async_computation.1 | async-start | bytes 2097152 | tf_op jit(solution)/shard_map/all_to_all | solution.py:127
  99.4 7.4 %collective-permute-start.3 = (bf16[256,2048]{1,0:T(8,128)(2,1)}, bf16[256,2048]{1,0:T(8,128)(2,1)}, u32[]{:S(2)}, u32[]{:S(2)}) collective-permute-start(bf16[256,2048]{1,0:T(8,128)(2,1)} %get-tuple-element.13.refs_0_), channel_id=1, source_target_pairs={{0,1},{1,0},{4,5},{5,4},{8,9},{9,8},{12,13},{13,12},{2,3},{3,2},{6... | collective-permute-start | bytes 3145736 | tf_op jit(solution)/shard_map/ppermute | solution.py:21
  99.4 50.1 %collective-permute-start.4 = (bf16[256,2048]{1,0:T(8,128)(2,1)}, bf16[256,2048]{1,0:T(8,128)(2,1)}, u32[]{:S(2)}, u32[]{:S(2)}) collective-permute-start(bf16[256,2048]{1,0:T(8,128)(2,1)} %get-tuple-element.13.refs_0_), channel_id=1, source_target_pairs={{0,4},{4,0},{1,5},{5,1},{8,12},{12,8},{9,13},{13,9},{2,6},{6,2},{3... | collective-permute-start | bytes 3145736 | tf_op jit(solution)/shard_map/ppermute | solution.py:21
  99.5 51.9 %collective-permute-start.5 = (bf16[256,2048]{1,0:T(8,128)(2,1)}, bf16[256,2048]{1,0:T(8,128)(2,1)}, u32[]{:S(2)}, u32[]{:S(2)}) collective-permute-start(bf16[256,2048]{1,0:T(8,128)(2,1)} %get-tuple-element.13.refs_0_), channel_id=1, source_target_pairs={{0,8},{8,0},{1,9},{9,1},{4,12},{12,4},{5,13},{13,5},{2,10},{10,2},... | collective-permute-start | bytes 3145736 | tf_op jit(solution)/shard_map/ppermute | solution.py:21
  173.3 1.0 copy-start
  174.3 7.9 %collective-permute-start.6 = (bf16[256,2048]{1,0:T(8,128)(2,1)}, bf16[256,2048]{1,0:T(8,128)(2,1)}, u32[]{:S(2)}, u32[]{:S(2)}) collective-permute-start(bf16[256,2048]{1,0:T(8,128)(2,1)} %get-tuple-element.17), channel_id=1, source_target_pairs={{0,1},{1,0},{4,5},{5,4},{8,9},{9,8},{12,13},{13,12},{2,3},{3,2},{6... | collective-permute-start | bytes 3145736 | tf_op jit(solution)/shard_map/ppermute | solution.py:21
  174.3 47.7 %collective-permute-start.7 = (bf16[256,2048]{1,0:T(8,128)(2,1)}, bf16[256,2048]{1,0:T(8,128)(2,1)}, u32[]{:S(2)}, u32[]{:S(2)}) collective-permute-start(bf16[256,2048]{1,0:T(8,128)(2,1)} %get-tuple-element.18), channel_id=1, source_target_pairs={{0,4},{4,0},{1,5},{5,1},{8,12},{12,8},{9,13},{13,9},{2,6},{6,2},{3... | collective-permute-start | bytes 3145736 | tf_op jit(solution)/shard_map/ppermute | solution.py:21
  174.3 51.2 %collective-permute-start.8 = (bf16[256,2048]{1,0:T(8,128)(2,1)}, bf16[256,2048]{1,0:T(8,128)(2,1)}, u32[]{:S(2)}, u32[]{:S(2)}) collective-permute-start(bf16[256,2048]{1,0:T(8,128)(2,1)} %get-tuple-element.19), channel_id=1, source_target_pairs={{0,8},{8,0},{1,9},{9,1},{4,12},{12,4},{5,13},{13,5},{2,10},{10,2},... | collective-permute-start | bytes 3145736 | tf_op jit(solution)/shard_map/ppermute | solution.py:21
  176.4 72.0 %collective-permute-start.10 = (bf16[16,8,64,128]{3,2,1,0:T(8,128)(2,1)}, bf16[16,8,64,128]{3,2,1,0:T(8,128)(2,1)}, u32[]{:S(2)}, u32[]{:S(2)}) collective-permute-start(bf16[16,8,64,128]{3,2,1,0:T(8,128)(2,1)} %get-tuple-element.23), channel_id=1, source_target_pairs={{0,2},{2,0},{1,3},{3,1},{4,6},{6,4},{5,7},{7,5},{8,10},{10,8},{9,1... | collective-permute-start | bytes 6291464 | tf_op jit(solution)/shard_map/ppermute | solution.py:21
  177.9 68.2 %all-to-all-start.2 = ((bf16[8,32,2048]{2,1,0:T(8,128)(2,1)}), bf16[8,32,2048]{2,1,0:T(8,128)(2,1)}, u32[]{:S(2)}, u32[]{:S(2)}) async-start(bf16[8,32,2048]{2,1,0:T(8,128)(2,1)} %bitcast.28), calls=%async_computation.2 | async-start | bytes 2097152 | tf_op jit(solution)/shard_map/all_to_all | solution.py:195
  241.2 46.4 %collective-permute-start.9 = (bf16[16,8,64,128]{3,2,1,0:T(8,128)(2,1)}, bf16[16,8,64,128]{3,2,1,0:T(8,128)(2,1)S(1)}, u32[]{:S(2)}, u32[]{:S(2)}) collective-permute-start(bf16[16,8,64,128]{3,2,1,0:T(8,128)(2,1)} %get-tuple-element.21), channel_id=1, source_target_pairs={{0,2},{2,0},{1,3},{3,1},{4,6},{6,4},{5,7},{7,5},{8,10},{10,8},{9,1... | collective-permute-start | bytes 6291464 | tf_op jit(solution)/shard_map/ppermute | solution.py:21
  248.4 39.2 %copy-start.1 = (f32[16,8,64,128]{3,2,1,0:T(8,128)S(1)}, f32[16,8,64,128]{3,2,1,0:T(8,128)}, u32[]{:S(2)}) copy-start(f32[16,8,64,128]{3,2,1,0:T(8,128)} %get-tuple-element.20) | copy-start | bytes 12582916

commit v2 on v1

v2 whole, which is shorter than its diff:
```python
import functools

import jax
import jax.numpy as jnp
from jax import lax
from jax.experimental import pallas as pl
from jax.experimental.pallas import tpu as pltpu
from jax.sharding import PartitionSpec as P

POS = ("feat", "sub")
VMEM_BYTES = 48 << 20


def swapped(block, axis, distance):
    count = lax.axis_size(axis)
    route = []
    for low in range(count):
        high = low | 1 << distance
        if high != low and high < count:
            route += [(low, high), (high, low)]
    return lax.ppermute(block, axis, route)


def pick_slots(lists_ref, layer, j, sources, picked, sizes, chosen):
    per_dev, slots, local, blk = sizes
    for place, s in enumerate(chosen):
        ref = sources[max(0, s - local + 1)]
        idx = lists_ref[(layer * per_dev + j) * slots + s]
        picked[:, place * blk : (place + 1) * blk] = ref[
            :, pl.ds(pl.multiple_of(idx * blk, blk), blk)
        ]


def near_kernel(sizes, layer, lists_ref, own_ref, partner_ref, w_ref, out_ref, picked):
    per_dev, slots, local, blk = sizes
    near = local + 1
    pick_slots(
        lists_ref, layer, pl.program_id(0), (own_ref, partner_ref), picked, sizes, range(near)
    )
    w = w_ref[:near].reshape(near * blk, blk)
    out_ref[...] = jnp.dot(picked[...], w, preferred_element_type=jnp.float32)


def with_far(sizes, layer, lists_ref, sources, near_ref, w_ref, picked):
    per_dev, slots, local, blk = sizes
    near = local + 1
    pick_slots(
        lists_ref,
        layer,
        pl.program_id(0),
        (None, None, *sources),
        picked,
        sizes,
        range(near, slots),
    )
    w = w_ref[near:].reshape((slots - near) * blk, blk)
    return jnp.tanh(near_ref[...] + jnp.dot(picked[...], w, preferred_element_type=jnp.float32))


def forward_kernel(sizes, far, lists_ref, *refs):
    sources, (near_ref, w_ref, tanh_ref, hidden_ref, picked) = refs[:far], refs[far:]
    out = with_far(sizes, 0, lists_ref, sources, near_ref, w_ref, picked)
    tanh_ref[...] = out
    hidden_ref[...] = out.astype(jnp.bfloat16)


def middle_kernel(sizes, levels, lists_ref, *refs):
    per_dev, slots, local, blk = sizes
    sources, refs = refs[: levels - 1], refs[levels - 1 :]
    near_ref, up_ref, w_ref, lifted_ref, grad_ref, own_sum = refs[:6]
    sent, picked, sums = refs[6 : 6 + levels], refs[6 + levels], refs[7 + levels :]
    j = pl.program_id(0)

    @pl.when(j == 0)
    def _():
        for ref in (own_sum, *sums):
            ref[...] = jnp.zeros_like(ref)

    out = with_far(sizes, 1, lists_ref, sources, near_ref, w_ref, picked)
    lifted_ref[...] = out.astype(jnp.bfloat16)
    grad = (up_ref[...].astype(jnp.float32) * (1.0 - out * out)).astype(jnp.bfloat16)
    grad_ref[...] = grad
    totals = (own_sum, *sums)
    for s in range(slots):
        term = lax.dot_general(
            grad, w_ref[s], (((1,), (1,)), ((), ())), preferred_element_type=jnp.float32
        )
        idx = lists_ref[(per_dev + j) * slots + s]
        where = pl.ds(pl.multiple_of(idx * blk, blk), blk)
        totals[max(0, s - local + 1)][:, where] += term

    @pl.when(j == per_dev - 1)
    def _():
        for ref, total in zip(sent, sums):
            ref[...] = total[...].astype(jnp.bfloat16)


def gradient_kernel(sizes, count, layer, dp, lists_ref, dp_ref, *refs):
    per_dev, slots, local, blk = sizes
    sources, refs = refs[:count], refs[count:]
    grad_ref, own_ref, picked = refs[0], refs[1], refs[-1]
    pick_slots(lists_ref, layer, pl.program_id(0), sources, picked, sizes, range(slots))
    grads = lax.dot_general(
        picked[...], grad_ref[...], (((0,), (0,)), ((), ())), preferred_element_type=jnp.float32
    )
    if dp == 2:
        blocks = grads.reshape(slots, 2, blk // 2, blk)
        low, high = blocks[:, 0], blocks[:, 1]
        first = dp_ref[0] == 0
        own_ref[...] = jnp.where(first, low, high)
        refs[2][...] = jnp.where(first, high, low).astype(jnp.bfloat16)
    else:
        own_ref[...] = grads.reshape(slots, blk, blk)


def halves_kernel(count, part, dp_ref, *refs):
    sources, (keep_ref, send_ref) = refs[:count], refs[count:]
    first = dp_ref[0] == 0
    for k, ref in enumerate(sources):
        turned = ref[...].T
        low, high = turned[:part], turned[part:]
        keep_ref[k] = jnp.where(first, low, high)
        send_ref[k] = jnp.where(first, high, low)


def merge_kernel(own_ref, other_ref, out_ref):
    out_ref[...] = own_ref[...] + other_ref[...].astype(jnp.float32)


def final_kernel(
    sizes, lists_ref, keep_ref, far_ref, grad_ref, far_grad_ref, _, out_ref, picked, grads
):
    per_dev, slots, local, blk = sizes
    rows = grad_ref.shape[0]
    part = blk // 2
    j = pl.program_id(0)
    grads[:rows] = grad_ref[...]
    grads[rows:] = far_grad_ref[...]
    for s in range(slots):
        source = max(0, s - local + 1)
        idx = lists_ref[j * slots + s]
        picked[s * part : (s + 1) * part, :rows] = keep_ref[source, idx]
        picked[s * part : (s + 1) * part, rows:] = far_ref[source, idx]
    total = jnp.dot(picked[...], grads[...], preferred_element_type=jnp.float32)
    out_ref[...] = total.reshape(slots, part, blk)


def per_device(snapshots, upstream, weights, block_lists):
    layers, per_dev, slots, blk, _ = weights.shape
    levels = lax.axis_size(POS).bit_length() - 1
    dp = lax.axis_size("dp")
    count = levels + 1
    far = levels - 1
    local = slots - levels
    near = local + 1
    position = lax.axis_index(POS)
    lists = (
        lax.dynamic_slice_in_dim(block_lists, position * per_dev, per_dev, 1) % per_dev
    ).reshape(-1)
    me_dp = lax.axis_index("dp").astype(jnp.int32).reshape(1)
    acts = lax.all_to_all(snapshots, POS, split_axis=1, concat_axis=0, tiled=True)
    upper = lax.all_to_all(upstream, POS, split_axis=1, concat_axis=0, tiled=True)
    rows, width = acts.shape
    sizes = (per_dev, slots, local, blk)
    part = blk // dp

    whole = pl.BlockSpec((rows, width), lambda j, *_: (0, 0))
    column = pl.BlockSpec((rows, blk), lambda j, *_: (0, j))

    def weight_spec(layer):
        return pl.BlockSpec((None, None, slots, blk, blk), lambda j, *_: (layer, j, 0, 0, 0))

    def array(shape, dtype):
        return jax.ShapeDtypeStruct(shape, dtype)

    def picks(number):
        return pltpu.VMEM((rows, number * blk), jnp.bfloat16)

    def with_partners(flat):
        return (flat, *(swapped(flat, POS, level) for level in range(levels)))

    def call(kernel, name, scalars, ins, in_specs, outs, out_specs, scratch, products, **more):
        flops = int(products * 2 * rows * per_dev * slots * blk * blk)
        moved = sum(x.size * x.dtype.itemsize for x in (*ins[: len(in_specs)], *outs))
        return pl.pallas_call(
            kernel,
            grid_spec=pltpu.PrefetchScalarGridSpec(
                num_scalar_prefetch=len(scalars),
                grid=(per_dev,),
                in_specs=in_specs,
                out_specs=out_specs,
                scratch_shapes=scratch,
            ),
            out_shape=outs,
            compiler_params=pltpu.CompilerParams(vmem_limit_bytes=VMEM_BYTES),
            cost_estimate=pl.CostEstimate(flops=flops, bytes_accessed=moved, transcendentals=0),
            name=name,
            **more,
        )(*scalars, *ins)

    full = array((rows, width), jnp.float32)
    half = array((rows, width), jnp.bfloat16)

    def near_part(layer, sources, name):
        return call(
            functools.partial(near_kernel, sizes, layer),
            name,
            [lists],
            [*sources[:2], weights],
            [whole, whole, weight_spec(layer)],
            [full],
            [column],
            [picks(near)],
            near / slots,
        )[0]

    def gradients(layer, sources, grad, name):
        if dp == 2:
            shape, kinds = (per_dev, slots, part, blk), (jnp.float32, jnp.bfloat16)
        else:
            shape, kinds = (per_dev, slots, blk, blk), (jnp.float32,)
        spec = pl.BlockSpec((None, *shape[1:]), lambda j, *_: (j, 0, 0, 0))
        return call(
            functools.partial(gradient_kernel, sizes, count, layer, dp),
            name,
            [lists, me_dp],
            [*sources, grad],
            [whole] * count + [column],
            [array(shape, kind) for kind in kinds],
            [spec] * len(kinds),
            [picks(slots)],
            1,
        )

    act_sources = with_partners(acts)
    near_one = near_part(0, act_sources, "layer_one_near")
    tanh_one, hidden = call(
        functools.partial(forward_kernel, sizes, far),
        "layer_one_far",
        [lists],
        [*act_sources[2:], near_one, weights],
        [whole] * far + [column, weight_spec(0)],
        [full, half],
        [column, column],
        [picks(slots - near)],
        0.25,
    )
    if dp == 2:
        turned = array((count, per_dev, part, rows), jnp.bfloat16)
        turned_spec = pl.BlockSpec((count, None, part, rows), lambda j, *_: (0, j, 0, 0))

    hidden_sources = with_partners(hidden)
    near_two = near_part(1, hidden_sources, "layer_two_near")
    if dp == 2:
        keep, send = call(
            functools.partial(halves_kernel, count, part),
            "snapshot_halves",
            [me_dp],
            list(lax.optimization_barrier((act_sources, near_two))[0]),
            [column] * count,
            [turned, turned],
            [turned_spec, turned_spec],
            [],
            0.1,
        )
        far_acts = swapped(send, "dp", 0)
        near_two, keep = lax.optimization_barrier((near_two, keep))
    middle = call(
        functools.partial(middle_kernel, sizes, levels),
        "layer_two_far",
        [lists],
        [*hidden_sources[2:], near_two, upper, weights],
        [whole] * far + [column, column, weight_spec(1)],
        [half, half, full] + [half] * levels,
        [column, column] + [whole] * count,
        [picks(slots - near)] + [pltpu.VMEM((rows, width), jnp.float32)] * levels,
        1.25,
    )
    lifted, grad_two, own_sum, sent = middle[0], middle[1], middle[2], middle[3:]
    received = [swapped(block, POS, level) for level, block in enumerate(sent)]
    second = gradients(1, hidden_sources, grad_two, "layer_two_gradient")
    lifted_rows = lax.all_to_all(lifted, POS, split_axis=0, concat_axis=1, tiled=True)

    total = own_sum
    for block in received:
        total = total + block.astype(jnp.float32)
    grad_one = (total * (1.0 - tanh_one * tanh_one)).astype(jnp.bfloat16)

    if dp != 2:
        first = gradients(0, act_sources, grad_one, "layer_one_gradient")
        grad_weights = lax.psum_scatter(
            jnp.stack([first[0], second[0]]), "dp", scatter_dimension=3, tiled=True
        )
        return (lifted_rows, grad_weights)

    far_grad = swapped(grad_one, "dp", 0)
    result = array((layers, per_dev, slots, part, blk), jnp.float32)
    part_spec = pl.BlockSpec((None, slots, part, blk), lambda j, *_: (j, 0, 0, 0))

    def result_spec(layer):
        return pl.BlockSpec((None, None, slots, part, blk), lambda j, *_: (layer, j, 0, 0, 0))

    merged = call(
        merge_kernel,
        "layer_two_sum",
        [],
        [second[0], swapped(second[1], "dp", 0)],
        [part_spec, part_spec],
        [result],
        [result_spec(1)],
        [],
        0,
    )[0]
    turned_whole = pl.BlockSpec(turned.shape, lambda j, *_: (0, 0, 0, 0))
    grad_weights = call(
        functools.partial(final_kernel, sizes),
        "layer_one_gradient",
        [lists],
        [keep, far_acts, grad_one, far_grad, merged],
        [turned_whole, turned_whole, column, column, pl.BlockSpec(memory_space=pl.ANY)],
        [result],
        [result_spec(0)],
        [
            pltpu.VMEM((slots * part, 2 * rows), jnp.bfloat16),
            pltpu.VMEM((2 * rows, blk), jnp.bfloat16),
        ],
        1,
        input_output_aliases={5: 0},
    )[0]
    return (lifted_rows, grad_weights)


def solution(mesh):
    in_specs = (
        P(("groups", "feat", "dp", "sub"), None),
        P(("groups", "feat", "dp", "sub"), None),
        P(None, ("feat", "sub"), None, None, None),
        P(),
    )
    out_specs = (
        P(("groups", "feat", "dp", "sub"), None),
        P("groups", ("feat", "sub"), None, "dp", None),
    )
    return jax.shard_map(
        per_device, mesh=mesh, in_specs=in_specs, out_specs=out_specs, check_vma=False
    )
```

time: 294 us -> 315 us (1.071)
  Pallas kernels: 51.2 us -> 100 us
  waiting for transfers between devices: 174 us -> 145 us
  other arithmetic: 8.76 us -> 3.97 us
    pallas_call x3 -> x8, Pallas kernels: 51.2 us -> 100 us  [call(): pl.pallas_call(kernel, grid_spec=pltpu.PrefetchScalarGridSpec(num_scalar_...]
    ppermute x11 -> x12, waiting for transfers between devices: 167 us -> 126 us  [swapped(): return lax.ppermute(block, axis, route)]
    all_to_all x1, waiting for transfers between devices: 3.36 us -> 15.6 us  [per_device(): lax.all_to_all(lifted, POS, split_axis=0, concat_axis=1, tiled=True)]
    another operation x3 -> x0, other arithmetic: 8.68 us -> none  [per_device(): jnp.stack([own + swapped(other, 'dp', 0).astype(jnp.float32) for own, oth...]
    convert_element_type x0 -> x1, other arithmetic: none -> 3.89 us  [per_device(): grad_one = (total * (1.0 - tanh_one * tanh_one)).astype(jnp.bfloat16)]
    ppermute x11 -> x12, starting transfers between devices: 11.2 us -> 11.5 us  [swapped(): return lax.ppermute(block, axis, route)]
  transfers between devices with their start and end apart: 13 -> 14, of which waited for: 9 -> 8; matrix products, arithmetic and copies ran while one was open for 2% -> 2% of each run, Pallas kernels for 10% -> 22%
where the time goes in v2:
time: 315 us; the launch traced here: 312 us
  waiting for transfers between devices  145 us (46%)
  Pallas kernels  100 us (32%)
  blocking collectives  32.7 us (10%)
  starting transfers between devices  20 us (6%)
  local copies, waits for them, and re-layouts  8.95 us (3%)
  other arithmetic  3.97 us (1%)
    ppermute x12, waiting for transfers between devices, swapped(): return lax.ppermute(block, axis, route)  126 us
    pallas_call x8, Pallas kernels, call(): pl.pallas_call(kernel, grid_spec=pltpu.PrefetchScalarGridSpec(num_scalar_...  100 us
    all_to_all x1, blocking collectives, per_device(): lax.all_to_all(snapshots, POS, split_axis=1, concat_axis=0, tiled=True)  32.7 us
    all_to_all x1, waiting for transfers between devices, per_device(): lax.all_to_all(lifted, POS, split_axis=0, concat_axis=1, tiled=True)  15.6 us
    ppermute x12, starting transfers between devices, swapped(): return lax.ppermute(block, axis, route)  11.5 us
  transfers between devices with their start and end apart: 14, of which 8 were waited for; matrix products, arithmetic and copies ran while one was open for 2% of the time, Pallas kernels for 22%

profile of v2, /device:TPU:0, one launch (start us, length us, event | category | flops | bytes accessed | tf_op | source)
XLA Modules:
  0.0 312.1 jit_solution(16327403334693723711)
XLA Ops:
  0.6 0.0 copy-start.4
  0.6 1.4 copy.20
  2.0 32.7 %all_to_all.57 = bf16[32,8,2048]{2,0,1:T(8,128)(2,1)S(1)} all-to-all(bf16[32,8,2048]{2,0,1:T(8,128)(2,1)S(1)} %bitcast.25), channel_id=1, replica_groups=mesh['groups'=2,'feat'=4,'dp'=2,'sub'=2] {'feat','sub'}, dimensions={1} | all-to-all | bytes 2097152 | tf_op jit(solution)/shard_map/all_to_all | solution.py:161
  34.7 0.0 collective-permute-start.2
  34.7 0.0 collective-permute-start.1
  34.7 1.9 collective-permute-start
  36.6 0.0 copy-done.4
  36.6 0.0 copy-start.5
  36.6 1.1 copy.19
  37.7 4.2 %all-to-all-start.1 = ((bf16[32,8,2048]{2,0,1:T(8,128)(2,1)}), bf16[32,8,2048]{2,0,1:T(8,128)(2,1)}, u32[]{:S(2)}, u32[]{:S(2)}) async-start(bf16[32,8,2048]{2,0,1:T(8,128)(2,1)} %bitcast.24), calls=%async_computation.1 | async-start | bytes 2097152 | tf_op jit(solution)/shard_map/all_to_all | solution.py:162
  41.9 0.0 copy-done.5
  42.0 0.1 add_select_fusion
  42.0 0.1 copy.10
  42.1 0.1 reshape.19.lists_ref
  42.2 0.0 collective-permute-done.2.partner_ref.refs_1_
  42.2 11.3 %layer_one_near.1.refs_2_ = f32[256,2048]{1,0:T(8,128)S(1)} custom-call(s32[256]{0:T(256)S(1)} %reshape.19.lists_ref, bf16[256,2048]{1,0:T(8,128)(2,1)S(1)} %bitcast.22, bf16[256,2048]{1,0:T(8,128)(2,1)S(1)} %collective-permute-done.2.partner_ref.refs_1_, bf16[2,16,8,128,128]{4,3,2,1,0:T(8,128)(2,1)} %refs_4_.1), custom_call_target="tpu_custom_call" | custom-call | flops 805306368 | bytes 12582912 | tf_op jit(solution)/shard_map/layer_one_near/pallas_call | solution.py:185
  53.6 0.0 copy-start
  53.6 1.3 copy-done
  54.9 28.4 %collective-permute-done.1.refs_1_.refs_3_ = bf16[256,2048]{1,0:T(8,128)(2,1)S(1)} collective-permute-done((bf16[256,2048]{1,0:T(8,128)(2,1)S(1)}, bf16[256,2048]{1,0:T(8,128)(2,1)S(1)}, u32[]{:S(2)}, u32[]{:S(2)}) %collective-permute-start.1) | collective-permute-done | bytes 1048608 | tf_op jit(solution)/shard_map/ppermute | solution.py:21
  83.3 0.0 collective-permute-done.refs_0_.refs_2_
  83.3 12.6 %layer_one_far.1 = (f32[256,2048]{1,0:T(8,128)S(1)}, bf16[256,2048]{1,0:T(8,128)(2,1)}) custom-call(s32[256]{0:T(256)S(1)} %reshape.19.lists_ref, bf16[256,2048]{1,0:T(8,128)(2,1)} %collective-permute-done.refs_0_.refs_2_, bf16[256,2048]{1,0:T(8,128)(2,1)S(1)} %collective-permute-done.1.refs_1_.refs_3_, f32[256,2048]{1,0:T(8,128)} %copy-done, ...), custom_call_target="tpu_custom_call" | custom-call | flops 268435456 | bytes 15728640 | tf_op jit(solution)/shard_map/layer_one_far/pallas_call | solution.py:185
  95.9 0.0 copy-start.3
  95.9 1.4 copy-done.3
  97.3 0.0 collective-permute-start.5
  97.3 0.6 collective-permute-start.4
  97.9 2.7 collective-permute-start.3
  100.6 0.0 collective-permute-done.5.partner_ref.refs_1_
  100.6 12.0 %layer_two_near.1.refs_2_ = f32[256,2048]{1,0:T(8,128)S(1)} custom-call(s32[256]{0:T(256)S(1)} %reshape.19.lists_ref, bf16[256,2048]{1,0:T(8,128)(2,1)} %get-tuple-element.20.own_ref.refs_0_, bf16[256,2048]{1,0:T(8,128)(2,1)} %collective-permute-done.5.partner_ref.refs_1_, bf16[2,16,8,128,128]{4,3,2,1,0:T(8,128)(2,1)} %refs_4_.1), custom_call_target="tpu_custom_call" | custom-call | flops 805306368 | bytes 12582912 | tf_op jit(solution)/shard_map/layer_two_near/pallas_call | solution.py:185
  112.6 0.0 copy-start.1
  112.7 1.3 copy-done.1
  114.0 10.2 %snapshot_halves.1 = (bf16[4,16,64,256]{3,2,1,0:T(8,128)(2,1)}, bf16[4,16,64,256]{3,2,1,0:T(8,128)(2,1)}) custom-call(s32[1]{0:T(128)} %bitcast.3.dp_ref, bf16[256,2048]{1,0:T(8,128)(2,1)S(1)} %bitcast.23, bf16[256,2048]{1,0:T(8,128)(2,1)S(1)} %collective-permute-done.2.partner_ref.refs_1_, bf16[256,2048]{1,0:T(8,128)(2,1)} %collective-permute-done.refs_0_.refs_2_, ...), custom_call_target="tpu_custom_call" | custom-call | flops 107374184 | bytes 8388608 | tf_op jit(solution)/shard_map/snapshot_halves/pallas_call | solution.py:185
  124.2 3.7 %all-to-all-done.1 = bf16[32,8,2048]{2,0,1:T(8,128)(2,1)} async-done(((bf16[32,8,2048]{2,0,1:T(8,128)(2,1)}), bf16[32,8,2048]{2,0,1:T(8,128)(2,1)}, u32[]{:S(2)}, u32[]{:S(2)}) %all-to-all-start.1) | async-done | bytes 1048608 | tf_op jit(solution)/shard_map/all_to_all | solution.py:162
  127.9 22.4 %collective-permute-done.4.refs_1_.refs_3_ = bf16[256,2048]{1,0:T(8,128)(2,1)} collective-permute-done((bf16[256,2048]{1,0:T(8,128)(2,1)}, bf16[256,2048]{1,0:T(8,128)(2,1)}, u32[]{:S(2)}, u32[]{:S(2)}) %collective-permute-start.4) | collective-permute-done | bytes 1048608 | tf_op jit(solution)/shard_map/ppermute | solution.py:21
  150.3 0.0 collective-permute-done.3.refs_0_.refs_2_
  150.3 18.0 %layer_two_far.1 = (bf16[256,2048]{1,0:T(8,128)(2,1)}, bf16[256,2048]{1,0:T(8,128)(2,1)S(1)}, f32[256,2048]{1,0:T(8,128)}, bf16[256,2048]{1,0:T(8,128)(2,1)}, bf...) custom-call(s32[256]{0:T(256)S(1)} %reshape.19.lists_ref, ...), custom_call_target="tpu_custom_call" | custom-call | flops 1342177280 | bytes 20971520 | tf_op jit(solution)/shard_map/layer_two_far/pallas_call | solution.py:185
  168.3 0.0 collective-permute-start.7
  168.4 0.0 collective-permute-start.8
  168.4 2.7 collective-permute-start.9
  171.1 13.2 %layer_two_gradient.1 = (f32[16,8,64,128]{3,2,1,0:T(8,128)}, bf16[16,8,64,128]{3,2,1,0:T(8,128)(2,1)}) custom-call(s32[256]{0:T(256)S(1)} %reshape.19.lists_ref, s32[1]{0:T(128)} %bitcast.3.dp_ref, bf16[256,2048]{1,0:T(8,128)(2,1)} %get-tuple-element.20.own_ref.refs_0_, bf16[256,2048]{1,0:T(8,128)(2,1)} %collective-permute-done.5.partner_ref.refs_1_, ...), custom_call_target="tpu_custom_call" | custom-call | flops 1073741824 | bytes 11534336 | tf_op jit(solution)/shard_map/layer_two_gradient/pallas_call | solution.py:185
  184.3 1.5 collective-permute-start.11
  185.7 0.5 collective-permute-start.6
  186.3 4.2 %all-to-all-start.2 = ((bf16[8,32,2048]{2,1,0:T(8,128)(2,1)}), bf16[8,32,2048]{2,1,0:T(8,128)(2,1)}, u32[]{:S(2)}, u32[]{:S(2)}) async-start(bf16[8,32,2048]{2,1,0:T(8,128)(2,1)} %bitcast.6), calls=%async_computation.2 | async-start | bytes 2097152 | tf_op jit(solution)/shard_map/all_to_all | solution.py:282
  190.5 0.0 collective-permute-done.7
  190.5 26.4 %collective-permute-done.8 = bf16[256,2048]{1,0:T(8,128)(2,1)} collective-permute-done((bf16[256,2048]{1,0:T(8,128)(2,1)}, bf16[256,2048]{1,0:T(8,128)(2,1)}, u32[]{:S(2)}, u32[]{:S(2)}) %collective-permute-start.8) | collective-permute-done | bytes 1048608 | tf_op jit(solution)/shard_map/ppermute | solution.py:21
  216.9 1.9 collective-permute-done.9
  218.8 3.9 %multiply_convert_fusion.grad_ref = bf16[256,2048]{1,0:T(8,128)(2,1)S(1)} fusion(f32[256,2048]{1,0:T(8,128)} %copy-done.3, bf16[256,2048]{1,0:T(8,128)(2,1)} %collective-permute-done.9, bf16[256,2048]{1,0:T(8,128)(2,1)} %collective-permute-done.8, f32[256,2048]{1,0:T(8,128)} %get-tuple-element.30, bf16[256,2048]{1,0:T(8,128)(2,1)} %collective-permute-done.7), kind=kLoop, calls=%fused_computation | loop fusion | flops 5242880 | bytes 8388608 | tf_op jit(solution)/shard_map/convert_element_type | solution.py:287
  222.7 1.6 collective-permute-start.10
  224.2 15.6 %all-to-all-done.2 = bf16[8,32,2048]{2,1,0:T(8,128)(2,1)} async-done(((bf16[8,32,2048]{2,1,0:T(8,128)(2,1)}), bf16[8,32,2048]{2,1,0:T(8,128)(2,1)}, u32[]{:S(2)}, u32[]{:S(2)}) %all-to-all-start.2) | async-done | bytes 1048608 | tf_op jit(solution)/shard_map/all_to_all | solution.py:282
  239.9 2.3 copy.16
  242.2 0.0 collective-permute-done.11.other_ref
  242.2 0.0 copy-start.2
  242.2 10.3 %layer_two_sum.1._ = f32[2,16,8,64,128]{4,3,2,1,0:T(8,128)} custom-call(f32[16,8,64,128]{3,2,1,0:T(8,128)} %get-tuple-element.36.own_ref, bf16[16,8,64,128]{3,2,1,0:T(8,128)(2,1)S(1)} %collective-permute-done.11.other_ref), custom_call_target="tpu_custom_call" | custom-call | bytes 14680064 | tf_op jit(solution)/shard_map/layer_two_sum/pallas_call | solution.py:185
  252.5 25.5 %collective-permute-done.6.far_ref = bf16[4,16,64,256]{3,2,1,0:T(8,128)(2,1)} collective-permute-done((bf16[4,16,64,256]{3,2,1,0:T(8,128)(2,1)}, bf16[4,16,64,256]{3,2,1,0:T(8,128)(2,1)}, u32[]{:S(2)}, u32[]{:S(2)}) %collective-permute-start.6) | collective-permute-done | bytes 2097184 | tf_op jit(solution)/shard_map/ppermute | solution.py:21
  278.0 21.4 %collective-permute-done.10.far_grad_ref = bf16[256,2048]{1,0:T(8,128)(2,1)} collective-permute-done((bf16[256,2048]{1,0:T(8,128)(2,1)S(1)}, bf16[256,2048]{1,0:T(8,128)(2,1)}, u32[]{:S(2)}, u32[]{:S(2)}) %collective-permute-start.10) | collective-permute-done | bytes 1048608 | tf_op jit(solution)/shard_map/ppermute | solution.py:21
  299.4 0.0 copy-done.2
  299.4 12.7 %layer_one_gradient.1 = f32[2,16,8,64,128]{4,3,2,1,0:T(8,128)} custom-call(s32[256]{0:T(256)S(1)} %reshape.19.lists_ref, bf16[4,16,64,256]{3,2,1,0:T(8,128)(2,1)S(1)} %copy-done.2, bf16[4,16,64,256]{3,2,1,0:T(8,128)(2,1)} %collective-permute-done.6.far_ref, bf16[256,2048]{1,0:T(8,128)(2,1)S(1)} %multiply_convert_fusion.grad_ref, ...), custom_call_target="tpu_custom_call", output_to_operand_aliasing={{}: (5, {})} | custom-call | flops 1073741824 | bytes 23068672 | tf_op jit(solution)/shard_map/layer_one_gradient/pallas_call | solution.py:185
Async XLA Ops:
  0.6 36.0 %copy-start.4 = (bf16[32,16384]{1,0:T(8,128)(2,1)S(1)}, bf16[32,16384]{1,0:T(8,128)(2,1)}, u32[]{:S(2)}) copy-start(bf16[32,16384]{1,0:T(8,128)(2,1)} %param.5) | copy-start | bytes 3145732
  34.7 7.5 %collective-permute-start.2 = (bf16[256,2048]{1,0:T(8,128)(2,1)S(1)}, bf16[256,2048]{1,0:T(8,128)(2,1)S(1)}, u32[]{:S(2)}, u32[]{:S(2)}) collective-permute-start(bf16[256,2048]{1,0:T(8,128)(2,1)S(1)} %bitcast.19), channel_id=1, source_target_pairs={{0,1},{1,0},{4,5},{5,4},{8,9},{9,8},{12,13},{13,12},{2,3},{3,2},{6... | collective-permute-start | bytes 3145736 | tf_op jit(solution)/shard_map/ppermute | solution.py:21
  34.7 48.5 %collective-permute-start.1 = (bf16[256,2048]{1,0:T(8,128)(2,1)S(1)}, bf16[256,2048]{1,0:T(8,128)(2,1)S(1)}, u32[]{:S(2)}, u32[]{:S(2)}) collective-permute-start(bf16[256,2048]{1,0:T(8,128)(2,1)S(1)} %bitcast.20), channel_id=1, source_target_pairs={{0,8},{8,0},{1,9},{9,1},{4,12},{12,4},{5,13},{13,5},{2,10},{10,2},... | collective-permute-start | bytes 3145736 | tf_op jit(solution)/shard_map/ppermute | solution.py:21
  34.7 48.5 %collective-permute-start = (bf16[256,2048]{1,0:T(8,128)(2,1)S(1)}, bf16[256,2048]{1,0:T(8,128)(2,1)}, u32[]{:S(2)}, u32[]{:S(2)}) collective-permute-start(bf16[256,2048]{1,0:T(8,128)(2,1)S(1)} %bitcast.21), channel_id=1, source_target_pairs={{0,4},{4,0},{1,5},{5,1},{8,12},{12,8},{9,13},{13,9},{2,6},{6,2},{3... | collective-permute-start | bytes 3145736 | tf_op jit(solution)/shard_map/ppermute | solution.py:21
  36.6 5.3 %copy-start.5 = (s32[2,128,8]{1,2,0:T(8,128)S(1)}, s32[2,128,8]{1,2,0:T(8,128)}, u32[]{:S(2)}) copy-start(s32[2,128,8]{1,2,0:T(8,128)} %param.7) | copy-start | bytes 24580
  37.7 90.2 %all-to-all-start.1 = ((bf16[32,8,2048]{2,0,1:T(8,128)(2,1)}), bf16[32,8,2048]{2,0,1:T(8,128)(2,1)}, u32[]{:S(2)}, u32[]{:S(2)}) async-start(bf16[32,8,2048]{2,0,1:T(8,128)(2,1)} %bitcast.24), calls=%async_computation.1 | async-start | bytes 2097152 | tf_op jit(solution)/shard_map/all_to_all | solution.py:162
  53.6 1.3 copy-start
  95.9 1.4 copy-start.3
  97.3 3.3 %collective-permute-start.5 = (bf16[256,2048]{1,0:T(8,128)(2,1)}, bf16[256,2048]{1,0:T(8,128)(2,1)}, u32[]{:S(2)}, u32[]{:S(2)}) collective-permute-start(bf16[256,2048]{1,0:T(8,128)(2,1)} %get-tuple-element.20.own_ref.refs_0_), channel_id=1, source_target_pairs={{0,1},{1,0},{4,5},{5,4},{8,9},{9,8},{12,13},{13,12},{2,3},{3,2},{6... | collective-permute-start | bytes 3145736 | tf_op jit(solution)/shard_map/ppermute | solution.py:21
  97.3 53.0 %collective-permute-start.4 = (bf16[256,2048]{1,0:T(8,128)(2,1)}, bf16[256,2048]{1,0:T(8,128)(2,1)}, u32[]{:S(2)}, u32[]{:S(2)}) collective-permute-start(bf16[256,2048]{1,0:T(8,128)(2,1)} %get-tuple-element.20.own_ref.refs_0_), channel_id=1, source_target_pairs={{0,8},{8,0},{1,9},{9,1},{4,12},{12,4},{5,13},{13,5},{2,10},{10,2},... | collective-permute-start | bytes 3145736 | tf_op jit(solution)/shard_map/ppermute | solution.py:21
  97.9 52.4 %collective-permute-start.3 = (bf16[256,2048]{1,0:T(8,128)(2,1)}, bf16[256,2048]{1,0:T(8,128)(2,1)}, u32[]{:S(2)}, u32[]{:S(2)}) collective-permute-start(bf16[256,2048]{1,0:T(8,128)(2,1)} %get-tuple-element.20.own_ref.refs_0_), channel_id=1, source_target_pairs={{0,4},{4,0},{1,5},{5,1},{8,12},{12,8},{9,13},{13,9},{2,6},{6,2},{3... | collective-permute-start | bytes 3145736 | tf_op jit(solution)/shard_map/ppermute | solution.py:21
  112.6 1.3 copy-start.1
  168.3 22.2 %collective-permute-start.7 = (bf16[256,2048]{1,0:T(8,128)(2,1)}, bf16[256,2048]{1,0:T(8,128)(2,1)}, u32[]{:S(2)}, u32[]{:S(2)}) collective-permute-start(bf16[256,2048]{1,0:T(8,128)(2,1)} %get-tuple-element.31), channel_id=1, source_target_pairs={{0,1},{1,0},{4,5},{5,4},{8,9},{9,8},{12,13},{13,12},{2,3},{3,2},{6... | collective-permute-start | bytes 3145736 | tf_op jit(solution)/shard_map/ppermute | solution.py:21
  168.4 48.5 %collective-permute-start.8 = (bf16[256,2048]{1,0:T(8,128)(2,1)}, bf16[256,2048]{1,0:T(8,128)(2,1)}, u32[]{:S(2)}, u32[]{:S(2)}) collective-permute-start(bf16[256,2048]{1,0:T(8,128)(2,1)} %get-tuple-element.32), channel_id=1, source_target_pairs={{0,4},{4,0},{1,5},{5,1},{8,12},{12,8},{9,13},{13,9},{2,6},{6,2},{3... | collective-permute-start | bytes 3145736 | tf_op jit(solution)/shard_map/ppermute | solution.py:21
  168.4 50.4 %collective-permute-start.9 = (bf16[256,2048]{1,0:T(8,128)(2,1)S(1)}, bf16[256,2048]{1,0:T(8,128)(2,1)}, u32[]{:S(2)}, u32[]{:S(2)}) collective-permute-start(bf16[256,2048]{1,0:T(8,128)(2,1)S(1)} %get-tuple-element.33), channel_id=1, source_target_pairs={{0,8},{8,0},{1,9},{9,1},{4,12},{12,4},{5,13},{13,5},{2,10},{10,2},... | collective-permute-start | bytes 3145736 | tf_op jit(solution)/shard_map/ppermute | solution.py:21
  184.3 58.0 %collective-permute-start.11 = (bf16[16,8,64,128]{3,2,1,0:T(8,128)(2,1)}, bf16[16,8,64,128]{3,2,1,0:T(8,128)(2,1)S(1)}, u32[]{:S(2)}, u32[]{:S(2)}) collective-permute-start(bf16[16,8,64,128]{3,2,1,0:T(8,128)(2,1)} %get-tuple-element.37), channel_id=1, source_target_pairs={{0,2},{2,0},{1,3},{3,1},{4,6},{6,4},{5,7},{7,5},{8,10},{10,8},{9,1... | collective-permute-start | bytes 6291464 | tf_op jit(solution)/shard_map/ppermute | solution.py:21
  185.7 92.3 %collective-permute-start.6 = (bf16[4,16,64,256]{3,2,1,0:T(8,128)(2,1)}, bf16[4,16,64,256]{3,2,1,0:T(8,128)(2,1)}, u32[]{:S(2)}, u32[]{:S(2)}) collective-permute-start(bf16[4,16,64,256]{3,2,1,0:T(8,128)(2,1)} %get-tuple-element.29), channel_id=1, source_target_pairs={{0,2},{2,0},{1,3},{3,1},{4,6},{6,4},{5,7},{7,5},{8,10},{10,8},{9,1... | collective-permute-start | bytes 6291464 | tf_op jit(solution)/shard_map/ppermute | solution.py:21
  186.3 53.6 %all-to-all-start.2 = ((bf16[8,32,2048]{2,1,0:T(8,128)(2,1)}), bf16[8,32,2048]{2,1,0:T(8,128)(2,1)}, u32[]{:S(2)}, u32[]{:S(2)}) async-start(bf16[8,32,2048]{2,1,0:T(8,128)(2,1)} %bitcast.6), calls=%async_computation.2 | async-start | bytes 2097152 | tf_op jit(solution)/shard_map/all_to_all | solution.py:282
  222.7 76.7 %collective-permute-start.10 = (bf16[256,2048]{1,0:T(8,128)(2,1)S(1)}, bf16[256,2048]{1,0:T(8,128)(2,1)}, u32[]{:S(2)}, u32[]{:S(2)}) collective-permute-start(bf16[256,2048]{1,0:T(8,128)(2,1)S(1)} %multiply_convert_fusion.grad_ref), channel_id=1, source_target_pairs={{0,2},{2,0},{1,3},{3,1},{4,6},{6,4},{5,7},{7,5},{8,10},{10,8},{9,1... | collective-permute-start | bytes 3145736 | tf_op jit(solution)/shard_map/ppermute | solution.py:21
  242.2 57.2 %copy-start.2 = (bf16[4,16,64,256]{3,2,1,0:T(8,128)(2,1)S(1)}, bf16[4,16,64,256]{3,2,1,0:T(8,128)(2,1)}, u32[]{:S(2)}) copy-start(bf16[4,16,64,256]{3,2,1,0:T(8,128)(2,1)} %get-tuple-element.28.keep_ref) | copy-start | bytes 6291460

commit v3 on v2

--- a/solution.py
+++ b/solution.py
@@ -31,44 +31,35 @@
         ]
 
 
-def near_kernel(sizes, layer, lists_ref, own_ref, partner_ref, w_ref, out_ref, picked):
-    per_dev, slots, local, blk = sizes
-    near = local + 1
-    pick_slots(
-        lists_ref, layer, pl.program_id(0), (own_ref, partner_ref), picked, sizes, range(near)
-    )
-    w = w_ref[:near].reshape(near * blk, blk)
-    out_ref[...] = jnp.dot(picked[...], w, preferred_element_type=jnp.float32)
-
-
-def with_far(sizes, layer, lists_ref, sources, near_ref, w_ref, picked):
-    per_dev, slots, local, blk = sizes
-    near = local + 1
-    pick_slots(
-        lists_ref,
-        layer,
-        pl.program_id(0),
-        (None, None, *sources),
-        picked,
-        sizes,
-        range(near, slots),
-    )
-    w = w_ref[near:].reshape((slots - near) * blk, blk)
-    return jnp.tanh(near_ref[...] + jnp.dot(picked[...], w, preferred_element_type=jnp.float32))
-
-
-def forward_kernel(sizes, far, lists_ref, *refs):
-    sources, (near_ref, w_ref, tanh_ref, hidden_ref, picked) = refs[:far], refs[far:]
-    out = with_far(sizes, 0, lists_ref, sources, near_ref, w_ref, picked)
+def layer(sizes, which, lists_ref, sources, w_ref, picked):
+    per_dev, slots, local, blk = sizes
+    pick_slots(lists_ref, which, pl.program_id(0), sources, picked, sizes, range(slots))
+    w = w_ref[...].reshape(slots * blk, blk)
+    return jnp.tanh(jnp.dot(picked[...], w, preferred_element_type=jnp.float32))
+
+
+def forward_kernel(sizes, count, part, lists_ref, dp_ref, *refs):
+    per_dev, slots, local, blk = sizes
+    sources, (w_ref, tanh_ref, hidden_ref), refs = refs[:count], refs[count : count + 3], refs[count + 3 :]
+    out = layer(sizes, 0, lists_ref, sources, w_ref, refs[-1])
     tanh_ref[...] = out
     hidden_ref[...] = out.astype(jnp.bfloat16)
+    if len(refs) == 3:
+        keep_ref, send_ref = refs[:2]
+        first = dp_ref[0] == 0
+        where = pl.ds(pl.multiple_of(pl.program_id(0) * blk, blk), blk)
+        for k, ref in enumerate(sources):
+            turned = ref[:, where].T
+            low, high = turned[:part], turned[part:]
+            keep_ref[k] = jnp.where(first, low, high)
+            send_ref[k] = jnp.where(first, high, low)
 
 
 def middle_kernel(sizes, levels, lists_ref, *refs):
     per_dev, slots, local, blk = sizes
-    sources, refs = refs[: levels - 1], refs[levels - 1 :]
-    near_ref, up_ref, w_ref, lifted_ref, grad_ref, own_sum = refs[:6]
-    sent, picked, sums = refs[6 : 6 + levels], refs[6 + levels], refs[7 + levels :]
+    sources, refs = refs[: levels + 1], refs[levels + 1 :]
+    up_ref, w_ref, lifted_ref, grad_ref, own_sum = refs[:5]
+    sent, picked, sums = refs[5 : 5 + levels], refs[5 + levels], refs[6 + levels :]
     j = pl.program_id(0)
 
     @pl.when(j == 0)
@@ -76,7 +67,7 @@
         for ref in (own_sum, *sums):
             ref[...] = jnp.zeros_like(ref)
 
-    out = with_far(sizes, 1, lists_ref, sources, near_ref, w_ref, picked)
+    out = layer(sizes, 1, lists_ref, sources, w_ref, picked)
     lifted_ref[...] = out.astype(jnp.bfloat16)
     grad = (up_ref[...].astype(jnp.float32) * (1.0 - out * out)).astype(jnp.bfloat16)
     grad_ref[...] = grad
@@ -111,16 +102,6 @@
         refs[2][...] = jnp.where(first, high, low).astype(jnp.bfloat16)
     else:
         own_ref[...] = grads.reshape(slots, blk, blk)
-
-
-def halves_kernel(count, part, dp_ref, *refs):
-    sources, (keep_ref, send_ref) = refs[:count], refs[count:]
-    first = dp_ref[0] == 0
-    for k, ref in enumerate(sources):
-        turned = ref[...].T
-        low, high = turned[:part], turned[part:]
-        keep_ref[k] = jnp.where(first, low, high)
-        send_ref[k] = jnp.where(first, high, low)
 
 
 def merge_kernel(own_ref, other_ref, out_ref):
@@ -150,9 +131,7 @@
     levels = lax.axis_size(POS).bit_length() - 1
     dp = lax.axis_size("dp")
     count = levels + 1
-    far = levels - 1
     local = slots - levels
-    near = local + 1
     position = lax.axis_index(POS)
     lists = (
         lax.dynamic_slice_in_dim(block_lists, position * per_dev, per_dev, 1) % per_dev
@@ -201,19 +180,6 @@
     full = array((rows, width), jnp.float32)
     half = array((rows, width), jnp.bfloat16)
 
-    def near_part(layer, sources, name):
-        return call(
-            functools.partial(near_kernel, sizes, layer),
-            name,
-            [lists],
-            [*sources[:2], weights],
-            [whole, whole, weight_spec(layer)],
-            [full],
-            [column],
-            [picks(near)],
-            near / slots,
-        )[0]
-
     def gradients(layer, sources, grad, name):
         if dp == 2:
             shape, kinds = (per_dev, slots, part, blk), (jnp.float32, jnp.bfloat16)
@@ -233,48 +199,34 @@
         )
 
     act_sources = with_partners(acts)
-    near_one = near_part(0, act_sources, "layer_one_near")
-    tanh_one, hidden = call(
-        functools.partial(forward_kernel, sizes, far),
-        "layer_one_far",
-        [lists],
-        [*act_sources[2:], near_one, weights],
-        [whole] * far + [column, weight_spec(0)],
-        [full, half],
-        [column, column],
-        [picks(slots - near)],
-        0.25,
-    )
+    turned = array((count, per_dev, part, rows), jnp.bfloat16)
+    turned_spec = pl.BlockSpec((count, None, part, rows), lambda j, *_: (0, j, 0, 0))
+    halves = 2 if dp == 2 else 0
+    tanh_one, hidden, *turned_acts = call(
+        functools.partial(forward_kernel, sizes, count, part),
+        "layer_one",
+        [lists, me_dp],
+        [*act_sources, weights],
+        [whole] * count + [weight_spec(0)],
+        [full, half] + [turned] * halves,
+        [column, column] + [turned_spec] * halves,
+        [picks(slots)],
+        1,
+    )
+    hidden_sources = with_partners(hidden)
     if dp == 2:
-        turned = array((count, per_dev, part, rows), jnp.bfloat16)
-        turned_spec = pl.BlockSpec((count, None, part, rows), lambda j, *_: (0, j, 0, 0))
-
-    hidden_sources = with_partners(hidden)
-    near_two = near_part(1, hidden_sources, "layer_two_near")
-    if dp == 2:
-        keep, send = call(
-            functools.partial(halves_kernel, count, part),
-            "snapshot_halves",
-            [me_dp],
-            list(lax.optimization_barrier((act_sources, near_two))[0]),
-            [column] * count,
-            [turned, turned],
-            [turned_spec, turned_spec],
-            [],
-            0.1,
-        )
-        far_acts = swapped(send, "dp", 0)
-        near_two, keep = lax.optimization_barrier((near_two, keep))
+        keep, far_acts = turned_acts[0], swapped(turned_acts[1], "dp", 0)
+        upper, far_acts = lax.optimization_barrier((upper, far_acts))
     middle = call(
         functools.partial(middle_kernel, sizes, levels),
-        "layer_two_far",
+        "layer_two",
         [lists],
-        [*hidden_sources[2:], near_two, upper, weights],
-        [whole] * far + [column, column, weight_spec(1)],
+        [*hidden_sources, upper, weights],
+        [whole] * count + [column, weight_spec(1)],
         [half, half, full] + [half] * levels,
         [column, column] + [whole] * count,
-        [picks(slots - near)] + [pltpu.VMEM((rows, width), jnp.float32)] * levels,
-        1.25,
+        [picks(slots)] + [pltpu.VMEM((rows, width), jnp.float32)] * levels,
+        2,
     )
     lifted, grad_two, own_sum, sent = middle[0], middle[1], middle[2], middle[3:]
     received = [swapped(block, POS, level) for level, block in enumerate(sent)]

time: 315 us -> 300 us (0.952)
  Pallas kernels: 100 us -> 69.4 us
  waiting for transfers between devices: 145 us -> 161 us
    all_to_all x1, waiting for transfers between devices: 3.71 us -> 45.2 us  [per_device(): lax.all_to_all(upstream, POS, split_axis=1, concat_axis=0, tiled=True)]
    pallas_call x8 -> x5, Pallas kernels: 100 us -> 69.4 us  [call(): pl.pallas_call(kernel, grid_spec=pltpu.PrefetchScalarGridSpec(num_scalar_...]
    ppermute x12, waiting for transfers between devices: 126 us -> 99.7 us  [swapped(): return lax.ppermute(block, axis, route)]
  transfers between devices with their start and end apart: 14 -> 14, of which waited for: 8 -> 8; matrix products, arithmetic and copies ran while one was open for 2% -> 3% of each run, Pallas kernels for 22% -> 8%
where the time goes in v3:
time: 300 us; the launch traced here: 298 us
  waiting for transfers between devices  161 us (54%)
  Pallas kernels  69.4 us (23%)
  blocking collectives  32.7 us (11%)
  starting transfers between devices  19.2 us (6%)
  local copies, waits for them, and re-layouts  10.8 us (4%)
  other arithmetic  3.97 us (1%)
    ppermute x12, waiting for transfers between devices, swapped(): return lax.ppermute(block, axis, route)  99.7 us
    pallas_call x5, Pallas kernels, call(): pl.pallas_call(kernel, grid_spec=pltpu.PrefetchScalarGridSpec(num_scalar_...  69.4 us
    all_to_all x1, waiting for transfers between devices, per_device(): lax.all_to_all(upstream, POS, split_axis=1, concat_axis=0, tiled=True)  45.2 us
    all_to_all x1, blocking collectives, per_device(): lax.all_to_all(snapshots, POS, split_axis=1, concat_axis=0, tiled=True)  32.7 us
    all_to_all x1, waiting for transfers between devices, per_device(): lax.all_to_all(lifted, POS, split_axis=0, concat_axis=1, tiled=True)  15.7 us
    ppermute x12, starting transfers between devices, swapped(): return lax.ppermute(block, axis, route)  10.7 us
  transfers between devices with their start and end apart: 14, of which 8 were waited for; matrix products, arithmetic and copies ran while one was open for 3% of the time, Pallas kernels for 8%

profile of v3, /device:TPU:0, one launch (start us, length us, event | category | flops | bytes accessed | tf_op | source)
XLA Modules:
  0.0 297.5 jit_solution(13242902214003920819)
XLA Ops:
  0.6 0.0 copy-start.11
  0.6 1.3 copy.20
  1.9 32.7 %all_to_all.57 = bf16[32,8,2048]{2,0,1:T(8,128)(2,1)S(1)} all-to-all(bf16[32,8,2048]{2,0,1:T(8,128)(2,1)S(1)} %bitcast.23), channel_id=1, replica_groups=mesh['groups'=2,'feat'=4,'dp'=2,'sub'=2] {'feat','sub'}, dimensions={1} | all-to-all | bytes 2097152 | tf_op jit(solution)/shard_map/all_to_all | solution.py:140
  34.7 0.0 collective-permute-start.2
  34.7 1.8 collective-permute-start.1
  36.5 0.0 collective-permute-start
  36.5 0.0 copy-done.11
  36.5 0.1 add_select_fusion
  36.6 0.1 copy.10
  36.6 0.1 reshape.19.lists_ref
  36.7 45.1 %collective-permute-done.2.refs_3_ = bf16[256,2048]{1,0:T(8,128)(2,1)S(1)} collective-permute-done((bf16[256,2048]{1,0:T(8,128)(2,1)S(1)}, bf16[256,2048]{1,0:T(8,128)(2,1)S(1)}, u32[]{:S(2)}, u32[]{:S(2)}) %collective-permute-start.2) | collective-permute-done | bytes 1048608 | tf_op jit(solution)/shard_map/ppermute | solution.py:21
  81.9 0.2 collective-permute-done.1.refs_2_
  82.1 0.0 copy-start.7
  82.1 1.0 copy-done.7
  83.0 0.0 collective-permute-done.refs_1_
  83.0 0.0 copy-start.8
  83.0 1.2 copy-done.8
  84.3 0.0 copy-start.9
  84.3 14.3 %layer_one.1 = (f32[256,2048]{1,0:T(8,128)}, bf16[256,2048]{1,0:T(8,128)(2,1)S(1)}, bf16[4,16,64,256]{3,2,1,0:T(8,128)(2,1)}, bf16[4,16,64,256]{3,2,1,0:T(8,128)(2,1)}) custom-call(s32[256]{0:T(256)S(1)} %reshape.19.lists_ref, s32[1]{0:T(128)} %bitcast.dp_ref, bf16[256,2048]{1,0:T(8,128)(2,1)S(1)} %bitcast.22, ...), custom_call_target="tpu_custom_call" | custom-call | flops 1073741824 | bytes 19922944 | tf_op jit(solution)/shard_map/layer_one/pallas_call | solution.py:164
  98.6 0.0 copy-start
  98.6 1.5 collective-permute-start.6
  100.1 0.0 copy-done.9
  100.1 1.1 copy.19
  101.2 4.2 %all-to-all-start.1 = ((bf16[32,8,2048]{2,0,1:T(8,128)(2,1)}), bf16[32,8,2048]{2,0,1:T(8,128)(2,1)}, u32[]{:S(2)}, u32[]{:S(2)}) async-start(bf16[32,8,2048]{2,0,1:T(8,128)(2,1)} %bitcast.17), calls=%async_computation.1 | async-start | bytes 2097152 | tf_op jit(solution)/shard_map/all_to_all | solution.py:141
  105.4 2.8 collective-permute-start.5
  108.2 1.5 collective-permute-start.4
  109.7 0.0 copy-done
  109.7 0.0 collective-permute-start.3
  109.7 45.2 %all-to-all-done.1 = bf16[32,8,2048]{2,0,1:T(8,128)(2,1)} async-done(((bf16[32,8,2048]{2,0,1:T(8,128)(2,1)}), bf16[32,8,2048]{2,0,1:T(8,128)(2,1)}, u32[]{:S(2)}, u32[]{:S(2)}) %all-to-all-start.1) | async-done | bytes 1048608 | tf_op jit(solution)/shard_map/all_to_all | solution.py:141
  155.0 0.0 collective-permute-done.6.far_ref
  155.0 0.0 copy-start.1
  155.0 21.9 %collective-permute-done.5.refs_3_ = bf16[256,2048]{1,0:T(8,128)(2,1)S(1)} collective-permute-done((bf16[256,2048]{1,0:T(8,128)(2,1)S(1)}, bf16[256,2048]{1,0:T(8,128)(2,1)S(1)}, u32[]{:S(2)}, u32[]{:S(2)}) %collective-permute-start.5) | collective-permute-done | bytes 1048608 | tf_op jit(solution)/shard_map/ppermute | solution.py:21
  176.9 0.0 copy-start.2
  176.9 0.0 collective-permute-done.4.refs_2_
  176.9 0.0 copy-start.4
  176.9 0.0 collective-permute-done.3.refs_1_
  176.9 1.0 copy-done.2
  177.8 0.3 copy-done.4
  178.2 19.5 %layer_two.1 = (bf16[256,2048]{1,0:T(8,128)(2,1)}, bf16[256,2048]{1,0:T(8,128)(2,1)S(1)}, f32[256,2048]{1,0:T(8,128)}, bf16[256,2048]{1,0:T(8,128)(2,1)}, bf16[2...) custom-call(s32[256]{0:T(256)S(1)} %reshape.19.lists_ref, bf16[256,2048]{1,0:T(8,128)(2,1)} %copy-done, ...), custom_call_target="tpu_custom_call" | custom-call | flops 2147483648 | bytes 20971520 | tf_op jit(solution)/shard_map/layer_two/pallas_call | solution.py:164
  197.7 0.1 collective-permute-start.7
  197.8 0.1 collective-permute-start.8
  197.9 1.8 collective-permute-start.9
  199.7 0.0 copy-done.1
  199.7 0.0 copy-start.3
  199.7 1.2 copy-done.3
  200.9 0.0 copy-start.5
  200.9 1.2 copy-done.5
  202.2 12.5 %layer_two_gradient.1 = (f32[16,8,64,128]{3,2,1,0:T(8,128)}, bf16[16,8,64,128]{3,2,1,0:T(8,128)(2,1)}) custom-call(s32[256]{0:T(256)S(1)} %reshape.19.lists_ref, s32[1]{0:T(128)} %bitcast.dp_ref, bf16[256,2048]{1,0:T(8,128)(2,1)S(1)} %copy-done.1, bf16[256,2048]{1,0:T(8,128)(2,1)} %collective-permute-done.3.refs_1_, bf16[256,2048]{1,0:T(8,128)(2,1)S(1)} %copy-done.5, ...), custom_call_target="tpu_custom_call" | custom-call | flops 1073741824 | bytes 11534336 | tf_op jit(solution)/shard_map/layer_two_gradient/pallas_call | solution.py:164
  214.6 0.5 collective-permute-start.11
  215.2 4.3 %all-to-all-start.2 = ((bf16[8,32,2048]{2,1,0:T(8,128)(2,1)}), bf16[8,32,2048]{2,1,0:T(8,128)(2,1)}, u32[]{:S(2)}, u32[]{:S(2)}) async-start(bf16[8,32,2048]{2,1,0:T(8,128)(2,1)} %bitcast.6), calls=%async_computation.2 | async-start | bytes 2097152 | tf_op jit(solution)/shard_map/all_to_all | solution.py:234
  219.4 0.0 collective-permute-done.7
  219.5 0.0 copy-start.10
  219.5 25.8 %collective-permute-done.8 = bf16[256,2048]{1,0:T(8,128)(2,1)} collective-permute-done((bf16[256,2048]{1,0:T(8,128)(2,1)}, bf16[256,2048]{1,0:T(8,128)(2,1)}, u32[]{:S(2)}, u32[]{:S(2)}) %collective-permute-start.8) | collective-permute-done | bytes 1048608 | tf_op jit(solution)/shard_map/ppermute | solution.py:21
  245.3 4.1 %collective-permute-done.9 = bf16[256,2048]{1,0:T(8,128)(2,1)} collective-permute-done((bf16[256,2048]{1,0:T(8,128)(2,1)}, bf16[256,2048]{1,0:T(8,128)(2,1)}, u32[]{:S(2)}, u32[]{:S(2)}) %collective-permute-start.9) | collective-permute-done | bytes 1048608 | tf_op jit(solution)/shard_map/ppermute | solution.py:21
  249.4 0.0 copy-done.10
  249.4 3.9 %multiply_convert_fusion.grad_ref = bf16[256,2048]{1,0:T(8,128)(2,1)S(1)} fusion(f32[256,2048]{1,0:T(8,128)} %get-tuple-element.26, bf16[256,2048]{1,0:T(8,128)(2,1)} %collective-permute-done.9, bf16[256,2048]{1,0:T(8,128)(2,1)} %collective-permute-done.8, f32[256,2048]{1,0:T(8,128)} %get-tuple-element.22, bf16[256,2048]{1,0:T(8,128)(2,1)} %copy-done.10), kind=kLoop, calls=%fused_computation | loop fusion | flops 5242880 | bytes 8388608 | tf_op jit(solution)/shard_map/convert_element_type | solution.py:239
  253.3 0.6 collective-permute-start.10
  253.9 15.7 %all-to-all-done.2 = bf16[8,32,2048]{2,1,0:T(8,128)(2,1)} async-done(((bf16[8,32,2048]{2,1,0:T(8,128)(2,1)}), bf16[8,32,2048]{2,1,0:T(8,128)(2,1)}, u32[]{:S(2)}, u32[]{:S(2)}) %all-to-all-start.2) | async-done | bytes 1048608 | tf_op jit(solution)/shard_map/all_to_all | solution.py:234
  269.6 2.3 copy.16
  271.9 0.0 collective-permute-done.11.other_ref
  271.9 10.3 %layer_two_sum.1._ = f32[2,16,8,64,128]{4,3,2,1,0:T(8,128)} custom-call(f32[16,8,64,128]{3,2,1,0:T(8,128)} %get-tuple-element.28.own_ref, bf16[16,8,64,128]{3,2,1,0:T(8,128)(2,1)S(1)} %collective-permute-done.11.other_ref), custom_call_target="tpu_custom_call" | custom-call | bytes 14680064 | tf_op jit(solution)/shard_map/layer_two_sum/pallas_call | solution.py:164
  282.2 2.6 collective-permute-done.10.far_grad_ref
  284.9 0.0 copy-done.6
  284.9 12.7 %layer_one_gradient.1 = f32[2,16,8,64,128]{4,3,2,1,0:T(8,128)} custom-call(s32[256]{0:T(256)S(1)} %reshape.19.lists_ref, bf16[4,16,64,256]{3,2,1,0:T(8,128)(2,1)S(1)} %copy-done.6, bf16[4,16,64,256]{3,2,1,0:T(8,128)(2,1)} %collective-permute-done.6.far_ref, bf16[256,2048]{1,0:T(8,128)(2,1)S(1)} %multiply_convert_fusion.grad_ref, ...), custom_call_target="tpu_custom_call", output_to_operand_aliasing={{}: (5, {})} | custom-call | flops 1073741824 | bytes 23068672 | tf_op jit(solution)/shard_map/layer_one_gradient/pallas_call | solution.py:164
  (1 shorter events, 0.0 us)
Async XLA Ops:
  0.6 35.9 %copy-start.11 = (s32[2,128,8]{1,2,0:T(8,128)S(1)}, s32[2,128,8]{1,2,0:T(8,128)}, u32[]{:S(2)}) copy-start(s32[2,128,8]{1,2,0:T(8,128)} %param.7) | copy-start | bytes 24580
  34.7 47.2 %collective-permute-start.2 = (bf16[256,2048]{1,0:T(8,128)(2,1)S(1)}, bf16[256,2048]{1,0:T(8,128)(2,1)S(1)}, u32[]{:S(2)}, u32[]{:S(2)}) collective-permute-start(bf16[256,2048]{1,0:T(8,128)(2,1)S(1)} %bitcast.19), channel_id=1, source_target_pairs={{0,8},{8,0},{1,9},{9,1},{4,12},{12,4},{5,13},{13,5},{2,10},{10,2},... | collective-permute-start | bytes 3145736 | tf_op jit(solution)/shard_map/ppermute | solution.py:21
  34.7 47.4 %collective-permute-start.1 = (bf16[256,2048]{1,0:T(8,128)(2,1)S(1)}, bf16[256,2048]{1,0:T(8,128)(2,1)S(1)}, u32[]{:S(2)}, u32[]{:S(2)}) collective-permute-start(bf16[256,2048]{1,0:T(8,128)(2,1)S(1)} %bitcast.20), channel_id=1, source_target_pairs={{0,4},{4,0},{1,5},{5,1},{8,12},{12,8},{9,13},{13,9},{2,6},{6,2},{3... | collective-permute-start | bytes 3145736 | tf_op jit(solution)/shard_map/ppermute | solution.py:21
  36.5 46.6 %collective-permute-start = (bf16[256,2048]{1,0:T(8,128)(2,1)S(1)}, bf16[256,2048]{1,0:T(8,128)(2,1)}, u32[]{:S(2)}, u32[]{:S(2)}) collective-permute-start(bf16[256,2048]{1,0:T(8,128)(2,1)S(1)} %bitcast.21), channel_id=1, source_target_pairs={{0,1},{1,0},{4,5},{5,4},{8,9},{9,8},{12,13},{13,12},{2,3},{3,2},{6... | collective-permute-start | bytes 3145736 | tf_op jit(solution)/shard_map/ppermute | solution.py:21
  82.1 1.0 copy-start.7
  83.0 1.2 copy-start.8
  84.3 15.8 %copy-start.9 = (bf16[32,16384]{1,0:T(8,128)(2,1)S(1)}, bf16[32,16384]{1,0:T(8,128)(2,1)}, u32[]{:S(2)}) copy-start(bf16[32,16384]{1,0:T(8,128)(2,1)} %param.5) | copy-start | bytes 3145732
  98.6 11.1 %copy-start = (bf16[256,2048]{1,0:T(8,128)(2,1)}, bf16[256,2048]{1,0:T(8,128)(2,1)S(1)}, u32[]{:S(2)}) copy-start(bf16[256,2048]{1,0:T(8,128)(2,1)S(1)} %get-tuple-element.16.refs_0_) | copy-start | bytes 3145732
  98.6 56.4 %collective-permute-start.6 = (bf16[4,16,64,256]{3,2,1,0:T(8,128)(2,1)}, bf16[4,16,64,256]{3,2,1,0:T(8,128)(2,1)}, u32[]{:S(2)}, u32[]{:S(2)}) collective-permute-start(bf16[4,16,64,256]{3,2,1,0:T(8,128)(2,1)} %get-tuple-element.17), channel_id=1, source_target_pairs={{0,2},{2,0},{1,3},{3,1},{4,6},{6,4},{5,7},{7,5},{8,10},{10,8},{9,1... | collective-permute-start | bytes 6291464 | tf_op jit(solution)/shard_map/ppermute | solution.py:21
  101.2 53.8 %all-to-all-start.1 = ((bf16[32,8,2048]{2,0,1:T(8,128)(2,1)}), bf16[32,8,2048]{2,0,1:T(8,128)(2,1)}, u32[]{:S(2)}, u32[]{:S(2)}) async-start(bf16[32,8,2048]{2,0,1:T(8,128)(2,1)} %bitcast.17), calls=%async_computation.1 | async-start | bytes 2097152 | tf_op jit(solution)/shard_map/all_to_all | solution.py:141
  105.4 71.4 %collective-permute-start.5 = (bf16[256,2048]{1,0:T(8,128)(2,1)S(1)}, bf16[256,2048]{1,0:T(8,128)(2,1)S(1)}, u32[]{:S(2)}, u32[]{:S(2)}) collective-permute-start(bf16[256,2048]{1,0:T(8,128)(2,1)S(1)} %get-tuple-element.16.refs_0_), channel_id=1, source_target_pairs={{0,8},{8,0},{1,9},{9,1},{4,12},{12,4},{5,13},{13,5},{2,10},{10,2},... | collective-permute-start | bytes 3145736 | tf_op jit(solution)/shard_map/ppermute | solution.py:21
  108.2 68.6 %collective-permute-start.4 = (bf16[256,2048]{1,0:T(8,128)(2,1)S(1)}, bf16[256,2048]{1,0:T(8,128)(2,1)S(1)}, u32[]{:S(2)}, u32[]{:S(2)}) collective-permute-start(bf16[256,2048]{1,0:T(8,128)(2,1)S(1)} %get-tuple-element.16.refs_0_), channel_id=1, source_target_pairs={{0,4},{4,0},{1,5},{5,1},{8,12},{12,8},{9,13},{13,9},{2,6},{6,2},{3... | collective-permute-start | bytes 3145736 | tf_op jit(solution)/shard_map/ppermute | solution.py:21
  109.7 67.1 %collective-permute-start.3 = (bf16[256,2048]{1,0:T(8,128)(2,1)S(1)}, bf16[256,2048]{1,0:T(8,128)(2,1)}, u32[]{:S(2)}, u32[]{:S(2)}) collective-permute-start(bf16[256,2048]{1,0:T(8,128)(2,1)S(1)} %get-tuple-element.16.refs_0_), channel_id=1, source_target_pairs={{0,1},{1,0},{4,5},{5,4},{8,9},{9,8},{12,13},{13,12},{2,3},{3,2},{6... | collective-permute-start | bytes 3145736 | tf_op jit(solution)/shard_map/ppermute | solution.py:21
  155.0 44.8 %copy-start.1 = (bf16[256,2048]{1,0:T(8,128)(2,1)S(1)}, bf16[256,2048]{1,0:T(8,128)(2,1)}, u32[]{:S(2)}) copy-start(bf16[256,2048]{1,0:T(8,128)(2,1)} %copy-done) | copy-start | bytes 3145732
  176.9 1.0 copy-start.2
  176.9 1.3 copy-start.4
  197.7 21.7 %collective-permute-start.7 = (bf16[256,2048]{1,0:T(8,128)(2,1)}, bf16[256,2048]{1,0:T(8,128)(2,1)S(1)}, u32[]{:S(2)}, u32[]{:S(2)}) collective-permute-start(bf16[256,2048]{1,0:T(8,128)(2,1)} %get-tuple-element.23), channel_id=1, source_target_pairs={{0,1},{1,0},{4,5},{5,4},{8,9},{9,8},{12,13},{13,12},{2,3},{3,2},{6... | collective-permute-start | bytes 3145736 | tf_op jit(solution)/shard_map/ppermute | solution.py:21
  197.8 47.5 %collective-permute-start.8 = (bf16[256,2048]{1,0:T(8,128)(2,1)}, bf16[256,2048]{1,0:T(8,128)(2,1)}, u32[]{:S(2)}, u32[]{:S(2)}) collective-permute-start(bf16[256,2048]{1,0:T(8,128)(2,1)} %get-tuple-element.24), channel_id=1, source_target_pairs={{0,4},{4,0},{1,5},{5,1},{8,12},{12,8},{9,13},{13,9},{2,6},{6,2},{3... | collective-permute-start | bytes 3145736 | tf_op jit(solution)/shard_map/ppermute | solution.py:21
  197.9 51.5 %collective-permute-start.9 = (bf16[256,2048]{1,0:T(8,128)(2,1)}, bf16[256,2048]{1,0:T(8,128)(2,1)}, u32[]{:S(2)}, u32[]{:S(2)}) collective-permute-start(bf16[256,2048]{1,0:T(8,128)(2,1)} %get-tuple-element.25), channel_id=1, source_target_pairs={{0,8},{8,0},{1,9},{9,1},{4,12},{12,4},{5,13},{13,5},{2,10},{10,2},... | collective-permute-start | bytes 3145736 | tf_op jit(solution)/shard_map/ppermute | solution.py:21
  199.7 1.2 copy-start.3
  200.9 1.2 copy-start.5
  214.6 57.3 %collective-permute-start.11 = (bf16[16,8,64,128]{3,2,1,0:T(8,128)(2,1)}, bf16[16,8,64,128]{3,2,1,0:T(8,128)(2,1)S(1)}, u32[]{:S(2)}, u32[]{:S(2)}) collective-permute-start(bf16[16,8,64,128]{3,2,1,0:T(8,128)(2,1)} %get-tuple-element.29), channel_id=1, source_target_pairs={{0,2},{2,0},{1,3},{3,1},{4,6},{6,4},{5,7},{7,5},{8,10},{10,8},{9,1... | collective-permute-start | bytes 6291464 | tf_op jit(solution)/shard_map/ppermute | solution.py:21
  215.2 54.4 %all-to-all-start.2 = ((bf16[8,32,2048]{2,1,0:T(8,128)(2,1)}), bf16[8,32,2048]{2,1,0:T(8,128)(2,1)}, u32[]{:S(2)}, u32[]{:S(2)}) async-start(bf16[8,32,2048]{2,1,0:T(8,128)(2,1)} %bitcast.6), calls=%async_computation.2 | async-start | bytes 2097152 | tf_op jit(solution)/shard_map/all_to_all | solution.py:234
  219.5 29.9 %copy-start.10 = (bf16[256,2048]{1,0:T(8,128)(2,1)}, bf16[256,2048]{1,0:T(8,128)(2,1)S(1)}, u32[]{:S(2)}) copy-start(bf16[256,2048]{1,0:T(8,128)(2,1)S(1)} %collective-permute-done.7) | copy-start | bytes 3145732
  253.3 31.6 %collective-permute-start.10 = (bf16[256,2048]{1,0:T(8,128)(2,1)S(1)}, bf16[256,2048]{1,0:T(8,128)(2,1)}, u32[]{:S(2)}, u32[]{:S(2)}) collective-permute-start(bf16[256,2048]{1,0:T(8,128)(2,1)S(1)} %multiply_convert_fusion.grad_ref), channel_id=1, source_target_pairs={{0,2},{2,0},{1,3},{3,1},{4,6},{6,4},{5,7},{7,5},{8,10},{10,8},{9,1... | collective-permute-start | bytes 3145736 | tf_op jit(solution)/shard_map/ppermute | solution.py:21
  271.9 12.9 %copy-start.6 = (bf16[4,16,64,256]{3,2,1,0:T(8,128)(2,1)S(1)}, bf16[4,16,64,256]{3,2,1,0:T(8,128)(2,1)}, u32[]{:S(2)}) copy-start(bf16[4,16,64,256]{3,2,1,0:T(8,128)(2,1)} %get-tuple-element.20.keep_ref) | copy-start | bytes 6291460

commit v4 on v3

--- a/solution.py
+++ b/solution.py
@@ -202,6 +202,7 @@
     turned = array((count, per_dev, part, rows), jnp.bfloat16)
     turned_spec = pl.BlockSpec((count, None, part, rows), lambda j, *_: (0, j, 0, 0))
     halves = 2 if dp == 2 else 0
+    lists, upper = lax.optimization_barrier((lists, upper))
     tanh_one, hidden, *turned_acts = call(
         functools.partial(forward_kernel, sizes, count, part),
         "layer_one",

time: 300 us -> 300 us (level)
  blocking collectives: 32.7 us -> 0 us
  waiting for transfers between devices: 161 us -> 183 us
  starting transfers between devices: 19.2 us -> 28.8 us
    all_to_all x1 -> x0, blocking collectives: 32.7 us -> none  [per_device(): lax.all_to_all(snapshots, POS, split_axis=1, concat_axis=0, tiled=True)]
    all_to_all x0 -> x1, waiting for transfers between devices: none -> 25.5 us  [per_device(): lax.all_to_all(snapshots, POS, split_axis=1, concat_axis=0, tiled=True)]
    all_to_all x0 -> x1, starting transfers between devices: none -> 6.33 us  [per_device(): lax.all_to_all(snapshots, POS, split_axis=1, concat_axis=0, tiled=True)]
    ppermute x12, starting transfers between devices: 10.7 us -> 14 us  [swapped(): return lax.ppermute(block, axis, route)]
  transfers between devices with their start and end apart: 14 -> 15, of which waited for: 8 -> 10; matrix products, arithmetic and copies ran while one was open for 3% -> 3% of each run, Pallas kernels for 8% -> 7%
where the time goes in v4:
time: 300 us; the launch traced here: 298 us
  waiting for transfers between devices  183 us (61%)
  Pallas kernels  67.8 us (23%)
  starting transfers between devices  28.8 us (10%)
  local copies, waits for them, and re-layouts  12.9 us (4%)
  other arithmetic  3.96 us (1%)
    ppermute x12, waiting for transfers between devices, swapped(): return lax.ppermute(block, axis, route)  98 us
    pallas_call x5, Pallas kernels, call(): pl.pallas_call(kernel, grid_spec=pltpu.PrefetchScalarGridSpec(num_scalar_...  67.8 us
    all_to_all x1, waiting for transfers between devices, per_device(): lax.all_to_all(upstream, POS, split_axis=1, concat_axis=0, tiled=True)  45 us
    all_to_all x1, waiting for transfers between devices, per_device(): lax.all_to_all(snapshots, POS, split_axis=1, concat_axis=0, tiled=True)  25.5 us
    all_to_all x1, waiting for transfers between devices, per_device(): lax.all_to_all(lifted, POS, split_axis=0, concat_axis=1, tiled=True)  14.9 us
    ppermute x12, starting transfers between devices, swapped(): return lax.ppermute(block, axis, route)  14 us
    unnamed x24, local copies, waits for them, and re-layouts  7.05 us
    all_to_all x1, starting transfers between devices, per_device(): lax.all_to_all(snapshots, POS, split_axis=1, concat_axis=0, tiled=True)  6.33 us
  transfers between devices with their start and end apart: 15, of which 10 were waited for; matrix products, arithmetic and copies ran while one was open for 3% of the time, Pallas kernels for 7%

profile of v4, /device:TPU:0, one launch (start us, length us, event | category | flops | bytes accessed | tf_op | source)
XLA Modules:
  0.0 297.7 jit_solution(15979592629430957690)
XLA Ops:
  0.6 0.0 copy-start.10
  0.6 2.4 copy.19
  3.0 6.3 %all-to-all-start.1 = ((bf16[32,8,2048]{2,0,1:T(8,128)(2,1)}), bf16[32,8,2048]{2,0,1:T(8,128)(2,1)S(1)}, u32[]{:S(2)}, u32[]{:S(2)}) async-start(bf16[32,8,2048]{2,0,1:T(8,128)(2,1)} %bitcast.17), calls=%async_computation.1 | async-start | bytes 2097152 | tf_op jit(solution)/shard_map/all_to_all | solution.py:140
  9.4 0.0 copy-done.10
  9.4 0.0 copy-start.11
  9.4 1.0 copy.20
  10.4 25.5 %all-to-all-done.1 = bf16[32,8,2048]{2,0,1:T(8,128)(2,1)S(1)} async-done(((bf16[32,8,2048]{2,0,1:T(8,128)(2,1)}), bf16[32,8,2048]{2,0,1:T(8,128)(2,1)S(1)}, u32[]{:S(2)}, u32[]{:S(2)}) %all-to-all-start.1) | async-done | bytes 1048608 | tf_op jit(solution)/shard_map/all_to_all | solution.py:140
  36.0 4.2 %all-to-all-start = ((bf16[32,8,2048]{2,0,1:T(8,128)(2,1)}), bf16[32,8,2048]{2,0,1:T(8,128)(2,1)}, u32[]{:S(2)}, u32[]{:S(2)}) async-start(bf16[32,8,2048]{2,0,1:T(8,128)(2,1)} %bitcast.18), calls=%async_computation | async-start | bytes 2097152 | tf_op jit(solution)/shard_map/all_to_all | solution.py:141
  40.2 2.8 collective-permute-start.2
  43.0 1.5 collective-permute-start.1
  44.5 0.0 collective-permute-start
  44.5 0.0 copy-done.11
  44.5 0.1 add_select_fusion
  44.6 0.1 copy.10
  44.7 0.1 reshape.19.lists_ref
  44.7 45.0 %all-to-all-done = bf16[32,8,2048]{2,0,1:T(8,128)(2,1)} async-done(((bf16[32,8,2048]{2,0,1:T(8,128)(2,1)}), bf16[32,8,2048]{2,0,1:T(8,128)(2,1)}, u32[]{:S(2)}, u32[]{:S(2)}) %all-to-all-start) | async-done | bytes 1048608 | tf_op jit(solution)/shard_map/all_to_all | solution.py:141
  89.7 21.9 %collective-permute-done.2.refs_3_ = bf16[256,2048]{1,0:T(8,128)(2,1)S(1)} collective-permute-done((bf16[256,2048]{1,0:T(8,128)(2,1)S(1)}, bf16[256,2048]{1,0:T(8,128)(2,1)S(1)}, u32[]{:S(2)}, u32[]{:S(2)}) %collective-permute-start.2) | collective-permute-done | bytes 1048608 | tf_op jit(solution)/shard_map/ppermute | solution.py:21
  111.6 0.0 collective-permute-done.1.refs_2_
  111.6 0.0 collective-permute-done.refs_1_
  111.6 14.3 %layer_one.1 = (f32[256,2048]{1,0:T(8,128)}, bf16[256,2048]{1,0:T(8,128)(2,1)S(1)}, bf16[4,16,64,256]{3,2,1,0:T(8,128)(2,1)}, bf16[4,16,64,256]{3,2,1,0:T(8,128)(2,1)}) custom-call(s32[256]{0:T(256)S(1)} %reshape.19.lists_ref, s32[1]{0:T(128)} %bitcast.2.dp_ref, bf16[256,2048]{1,0:T(8,128)(2,1)S(1)} %bitcast.22, ...), custom_call_target="tpu_custom_call" | custom-call | flops 1073741824 | bytes 19922944 | tf_op jit(solution)/shard_map/layer_one/pallas_call | solution.py:164
  125.9 0.0 copy-start
  125.9 1.5 collective-permute-start.6
  127.4 0.0 collective-permute-start.5
  127.4 1.8 collective-permute-start.4
  129.2 0.0 collective-permute-start.3
  129.2 44.1 %collective-permute-done.6.far_ref = bf16[4,16,64,256]{3,2,1,0:T(8,128)(2,1)S(1)} collective-permute-done((bf16[4,16,64,256]{3,2,1,0:T(8,128)(2,1)}, bf16[4,16,64,256]{3,2,1,0:T(8,128)(2,1)S(1)}, u32[]{:S(2)}, u32[]{:S(2)}) %collective-permute-start.6) | collective-permute-done | bytes 2097184 | tf_op jit(solution)/shard_map/ppermute | solution.py:21
  173.3 0.0 copy-start.9
  173.3 1.0 collective-permute-done.5.refs_3_
  174.3 0.0 copy-start.2
  174.4 0.2 collective-permute-done.4.refs_2_
  174.5 0.2 copy-done.9
  174.7 0.0 copy-start.4
  174.7 0.0 collective-permute-done.3.refs_1_
  174.7 0.0 copy-done
  174.7 0.6 copy-done.2
  175.3 0.4 copy-done.4
  175.7 0.0 copy-start.6
  175.7 1.0 copy-done.6
  176.7 19.2 %layer_two.1 = (bf16[256,2048]{1,0:T(8,128)(2,1)}, bf16[256,2048]{1,0:T(8,128)(2,1)S(1)}, f32[256,2048]{1,0:T(8,128)}, bf16[256,2048]{1,0:T(8,128)(2,1)}, bf16[2...) custom-call(s32[256]{0:T(256)S(1)} %reshape.19.lists_ref, bf16[256,2048]{1,0:T(8,128)(2,1)} %copy-done, ...), custom_call_target="tpu_custom_call" | custom-call | flops 2147483648 | bytes 20971520 | tf_op jit(solution)/shard_map/layer_two/pallas_call | solution.py:164
  195.9 0.0 collective-permute-start.7
  195.9 0.1 collective-permute-start.8
  196.0 2.7 collective-permute-start.9
  198.7 0.0 copy-start.1
  198.7 1.2 copy-done.1
  199.9 0.0 copy-start.3
  199.9 1.2 copy-done.3
  201.1 0.0 copy-start.5
  201.1 1.2 copy-done.5
  202.3 1.2 copy-done.7
  203.6 11.2 %layer_two_gradient.1 = (f32[16,8,64,128]{3,2,1,0:T(8,128)}, bf16[16,8,64,128]{3,2,1,0:T(8,128)(2,1)}) custom-call(s32[256]{0:T(256)S(1)} %reshape.19.lists_ref, s32[1]{0:T(128)} %bitcast.2.dp_ref, bf16[256,2048]{1,0:T(8,128)(2,1)S(1)} %copy-done.1, bf16[256,2048]{1,0:T(8,128)(2,1)S(1)} %copy-done.7, bf16[256,2048]{1,0:T(8,128)(2,1)S(1)} %copy-done.5, ...), custom_call_target="tpu_custom_call" | custom-call | flops 1073741824 | bytes 11534336 | tf_op jit(solution)/shard_map/layer_two_gradient/pallas_call | solution.py:164
  214.8 1.0 collective-permute-start.11
  215.8 4.2 %all-to-all-start.2 = ((bf16[8,32,2048]{2,1,0:T(8,128)(2,1)}), bf16[8,32,2048]{2,1,0:T(8,128)(2,1)}, u32[]{:S(2)}, u32[]{:S(2)}) async-start(bf16[8,32,2048]{2,1,0:T(8,128)(2,1)} %bitcast.6), calls=%async_computation.2 | async-start | bytes 2097152 | tf_op jit(solution)/shard_map/all_to_all | solution.py:235
  220.0 0.0 collective-permute-done.7
  220.1 24.4 %collective-permute-done.8 = bf16[256,2048]{1,0:T(8,128)(2,1)} collective-permute-done((bf16[256,2048]{1,0:T(8,128)(2,1)}, bf16[256,2048]{1,0:T(8,128)(2,1)}, u32[]{:S(2)}, u32[]{:S(2)}) %collective-permute-start.8) | collective-permute-done | bytes 1048608 | tf_op jit(solution)/shard_map/ppermute | solution.py:21
  244.5 1.5 collective-permute-done.9
  246.0 3.9 %multiply_convert_fusion.grad_ref = bf16[256,2048]{1,0:T(8,128)(2,1)S(1)} fusion(f32[256,2048]{1,0:T(8,128)} %get-tuple-element.30, bf16[256,2048]{1,0:T(8,128)(2,1)} %collective-permute-done.9, bf16[256,2048]{1,0:T(8,128)(2,1)} %collective-permute-done.8, f32[256,2048]{1,0:T(8,128)} %get-tuple-element.26, bf16[256,2048]{1,0:T(8,128)(2,1)} %collective-permute-done.7), kind=kLoop, calls=%fused_computation | loop fusion | flops 5242880 | bytes 8388608 | tf_op jit(solution)/shard_map/convert_element_type | solution.py:240
  249.9 2.7 collective-permute-start.10
  252.5 14.9 %all-to-all-done.2 = bf16[8,32,2048]{2,1,0:T(8,128)(2,1)} async-done(((bf16[8,32,2048]{2,1,0:T(8,128)(2,1)}), bf16[8,32,2048]{2,1,0:T(8,128)(2,1)}, u32[]{:S(2)}, u32[]{:S(2)}) %all-to-all-start.2) | async-done | bytes 1048608 | tf_op jit(solution)/shard_map/all_to_all | solution.py:235
  267.5 2.3 copy.16
  269.8 0.0 collective-permute-done.11.other_ref
  269.8 10.3 %layer_two_sum.1._ = f32[2,16,8,64,128]{4,3,2,1,0:T(8,128)} custom-call(f32[16,8,64,128]{3,2,1,0:T(8,128)} %get-tuple-element.32.own_ref, bf16[16,8,64,128]{3,2,1,0:T(8,128)(2,1)S(1)} %collective-permute-done.11.other_ref), custom_call_target="tpu_custom_call" | custom-call | bytes 14680064 | tf_op jit(solution)/shard_map/layer_two_sum/pallas_call | solution.py:164
  280.1 4.9 %collective-permute-done.10.far_grad_ref = bf16[256,2048]{1,0:T(8,128)(2,1)} collective-permute-done((bf16[256,2048]{1,0:T(8,128)(2,1)S(1)}, bf16[256,2048]{1,0:T(8,128)(2,1)}, u32[]{:S(2)}, u32[]{:S(2)}) %collective-permute-start.10) | collective-permute-done | bytes 1048608 | tf_op jit(solution)/shard_map/ppermute | solution.py:21
  285.0 0.0 copy-done.8
  285.0 12.7 %layer_one_gradient.1 = f32[2,16,8,64,128]{4,3,2,1,0:T(8,128)} custom-call(s32[256]{0:T(256)S(1)} %reshape.19.lists_ref, bf16[4,16,64,256]{3,2,1,0:T(8,128)(2,1)S(1)} %copy-done.8, bf16[4,16,64,256]{3,2,1,0:T(8,128)(2,1)} %copy-done.9, bf16[256,2048]{1,0:T(8,128)(2,1)S(1)} %multiply_convert_fusion.grad_ref, ...), custom_call_target="tpu_custom_call", output_to_operand_aliasing={{}: (5, {})} | custom-call | flops 1073741824 | bytes 23068672 | tf_op jit(solution)/shard_map/layer_one_gradient/pallas_call | solution.py:164
  (2 shorter events, 0.0 us)
Async XLA Ops:
  0.6 8.7 %copy-start.10 = (bf16[32,16384]{1,0:T(8,128)(2,1)S(1)}, bf16[32,16384]{1,0:T(8,128)(2,1)}, u32[]{:S(2)}) copy-start(bf16[32,16384]{1,0:T(8,128)(2,1)} %param.5) | copy-start | bytes 3145732
  3.0 32.9 %all-to-all-start.1 = ((bf16[32,8,2048]{2,0,1:T(8,128)(2,1)}), bf16[32,8,2048]{2,0,1:T(8,128)(2,1)S(1)}, u32[]{:S(2)}, u32[]{:S(2)}) async-start(bf16[32,8,2048]{2,0,1:T(8,128)(2,1)} %bitcast.17), calls=%async_computation.1 | async-start | bytes 2097152 | tf_op jit(solution)/shard_map/all_to_all | solution.py:140
  9.4 35.1 %copy-start.11 = (s32[2,128,8]{1,2,0:T(8,128)S(1)}, s32[2,128,8]{1,2,0:T(8,128)}, u32[]{:S(2)}) copy-start(s32[2,128,8]{1,2,0:T(8,128)} %param.7) | copy-start | bytes 24580
  36.0 53.8 %all-to-all-start = ((bf16[32,8,2048]{2,0,1:T(8,128)(2,1)}), bf16[32,8,2048]{2,0,1:T(8,128)(2,1)}, u32[]{:S(2)}, u32[]{:S(2)}) async-start(bf16[32,8,2048]{2,0,1:T(8,128)(2,1)} %bitcast.18), calls=%async_computation | async-start | bytes 2097152 | tf_op jit(solution)/shard_map/all_to_all | solution.py:141
  40.2 71.4 %collective-permute-start.2 = (bf16[256,2048]{1,0:T(8,128)(2,1)S(1)}, bf16[256,2048]{1,0:T(8,128)(2,1)S(1)}, u32[]{:S(2)}, u32[]{:S(2)}) collective-permute-start(bf16[256,2048]{1,0:T(8,128)(2,1)S(1)} %bitcast.19), channel_id=1, source_target_pairs={{0,8},{8,0},{1,9},{9,1},{4,12},{12,4},{5,13},{13,5},{2,10},{10,2},... | collective-permute-start | bytes 3145736 | tf_op jit(solution)/shard_map/ppermute | solution.py:21
  43.0 68.6 %collective-permute-start.1 = (bf16[256,2048]{1,0:T(8,128)(2,1)S(1)}, bf16[256,2048]{1,0:T(8,128)(2,1)S(1)}, u32[]{:S(2)}, u32[]{:S(2)}) collective-permute-start(bf16[256,2048]{1,0:T(8,128)(2,1)S(1)} %bitcast.20), channel_id=1, source_target_pairs={{0,4},{4,0},{1,5},{5,1},{8,12},{12,8},{9,13},{13,9},{2,6},{6,2},{3... | collective-permute-start | bytes 3145736 | tf_op jit(solution)/shard_map/ppermute | solution.py:21
  44.5 67.1 %collective-permute-start = (bf16[256,2048]{1,0:T(8,128)(2,1)S(1)}, bf16[256,2048]{1,0:T(8,128)(2,1)}, u32[]{:S(2)}, u32[]{:S(2)}) collective-permute-start(bf16[256,2048]{1,0:T(8,128)(2,1)S(1)} %bitcast.21), channel_id=1, source_target_pairs={{0,1},{1,0},{4,5},{5,4},{8,9},{9,8},{12,13},{13,12},{2,3},{3,2},{6... | collective-permute-start | bytes 3145736 | tf_op jit(solution)/shard_map/ppermute | solution.py:21
  125.9 48.8 %copy-start = (bf16[256,2048]{1,0:T(8,128)(2,1)}, bf16[256,2048]{1,0:T(8,128)(2,1)S(1)}, u32[]{:S(2)}) copy-start(bf16[256,2048]{1,0:T(8,128)(2,1)S(1)} %get-tuple-element.19.refs_0_) | copy-start | bytes 3145732
  125.9 47.4 %collective-permute-start.6 = (bf16[4,16,64,256]{3,2,1,0:T(8,128)(2,1)}, bf16[4,16,64,256]{3,2,1,0:T(8,128)(2,1)S(1)}, u32[]{:S(2)}, u32[]{:S(2)}) collective-permute-start(bf16[4,16,64,256]{3,2,1,0:T(8,128)(2,1)} %get-tuple-element.21), channel_id=1, source_target_pairs={{0,2},{2,0},{1,3},{3,1},{4,6},{6,4},{5,7},{7,5},{8,10},{10,8},{9,1... | collective-permute-start | bytes 6291464 | tf_op jit(solution)/shard_map/ppermute | solution.py:21
  127.4 46.9 %collective-permute-start.5 = (bf16[256,2048]{1,0:T(8,128)(2,1)S(1)}, bf16[256,2048]{1,0:T(8,128)(2,1)S(1)}, u32[]{:S(2)}, u32[]{:S(2)}) collective-permute-start(bf16[256,2048]{1,0:T(8,128)(2,1)S(1)} %get-tuple-element.19.refs_0_), channel_id=1, source_target_pairs={{0,8},{8,0},{1,9},{9,1},{4,12},{12,4},{5,13},{13,5},{2,10},{10,2},... | collective-permute-start | bytes 3145736 | tf_op jit(solution)/shard_map/ppermute | solution.py:21
  127.4 47.1 %collective-permute-start.4 = (bf16[256,2048]{1,0:T(8,128)(2,1)S(1)}, bf16[256,2048]{1,0:T(8,128)(2,1)S(1)}, u32[]{:S(2)}, u32[]{:S(2)}) collective-permute-start(bf16[256,2048]{1,0:T(8,128)(2,1)S(1)} %get-tuple-element.19.refs_0_), channel_id=1, source_target_pairs={{0,4},{4,0},{1,5},{5,1},{8,12},{12,8},{9,13},{13,9},{2,6},{6,2},{3... | collective-permute-start | bytes 3145736 | tf_op jit(solution)/shard_map/ppermute | solution.py:21
  129.2 45.5 %collective-permute-start.3 = (bf16[256,2048]{1,0:T(8,128)(2,1)S(1)}, bf16[256,2048]{1,0:T(8,128)(2,1)S(1)}, u32[]{:S(2)}, u32[]{:S(2)}) collective-permute-start(bf16[256,2048]{1,0:T(8,128)(2,1)S(1)} %get-tuple-element.19.refs_0_), channel_id=1, source_target_pairs={{0,1},{1,0},{4,5},{5,4},{8,9},{9,8},{12,13},{13,12},{2,3},{3,2},{6... | collective-permute-start | bytes 3145736 | tf_op jit(solution)/shard_map/ppermute | solution.py:21
  173.3 1.4 copy-start.9
  174.3 1.0 copy-start.2
  174.7 1.0 copy-start.4
  175.7 1.0 copy-start.6
  195.9 24.1 %collective-permute-start.7 = (bf16[256,2048]{1,0:T(8,128)(2,1)}, bf16[256,2048]{1,0:T(8,128)(2,1)}, u32[]{:S(2)}, u32[]{:S(2)}) collective-permute-start(bf16[256,2048]{1,0:T(8,128)(2,1)} %get-tuple-element.27), channel_id=1, source_target_pairs={{0,1},{1,0},{4,5},{5,4},{8,9},{9,8},{12,13},{13,12},{2,3},{3,2},{6... | collective-permute-start | bytes 3145736 | tf_op jit(solution)/shard_map/ppermute | solution.py:21
  195.9 48.6 %collective-permute-start.8 = (bf16[256,2048]{1,0:T(8,128)(2,1)}, bf16[256,2048]{1,0:T(8,128)(2,1)}, u32[]{:S(2)}, u32[]{:S(2)}) collective-permute-start(bf16[256,2048]{1,0:T(8,128)(2,1)} %get-tuple-element.28), channel_id=1, source_target_pairs={{0,4},{4,0},{1,5},{5,1},{8,12},{12,8},{9,13},{13,9},{2,6},{6,2},{3... | collective-permute-start | bytes 3145736 | tf_op jit(solution)/shard_map/ppermute | solution.py:21
  196.0 50.0 %collective-permute-start.9 = (bf16[256,2048]{1,0:T(8,128)(2,1)S(1)}, bf16[256,2048]{1,0:T(8,128)(2,1)}, u32[]{:S(2)}, u32[]{:S(2)}) collective-permute-start(bf16[256,2048]{1,0:T(8,128)(2,1)S(1)} %get-tuple-element.29), channel_id=1, source_target_pairs={{0,8},{8,0},{1,9},{9,1},{4,12},{12,4},{5,13},{13,5},{2,10},{10,2},... | collective-permute-start | bytes 3145736 | tf_op jit(solution)/shard_map/ppermute | solution.py:21
  198.7 1.2 copy-start.1
  199.9 1.2 copy-start.3
  201.1 1.2 copy-start.5
  202.3 1.2 copy-start.7
  214.8 55.0 %collective-permute-start.11 = (bf16[16,8,64,128]{3,2,1,0:T(8,128)(2,1)}, bf16[16,8,64,128]{3,2,1,0:T(8,128)(2,1)S(1)}, u32[]{:S(2)}, u32[]{:S(2)}) collective-permute-start(bf16[16,8,64,128]{3,2,1,0:T(8,128)(2,1)} %get-tuple-element.33), channel_id=1, source_target_pairs={{0,2},{2,0},{1,3},{3,1},{4,6},{6,4},{5,7},{7,5},{8,10},{10,8},{9,1... | collective-permute-start | bytes 6291464 | tf_op jit(solution)/shard_map/ppermute | solution.py:21
  215.8 51.7 %all-to-all-start.2 = ((bf16[8,32,2048]{2,1,0:T(8,128)(2,1)}), bf16[8,32,2048]{2,1,0:T(8,128)(2,1)}, u32[]{:S(2)}, u32[]{:S(2)}) async-start(bf16[8,32,2048]{2,1,0:T(8,128)(2,1)} %bitcast.6), calls=%async_computation.2 | async-start | bytes 2097152 | tf_op jit(solution)/shard_map/all_to_all | solution.py:235
  249.9 35.1 %collective-permute-start.10 = (bf16[256,2048]{1,0:T(8,128)(2,1)S(1)}, bf16[256,2048]{1,0:T(8,128)(2,1)}, u32[]{:S(2)}, u32[]{:S(2)}) collective-permute-start(bf16[256,2048]{1,0:T(8,128)(2,1)S(1)} %multiply_convert_fusion.grad_ref), channel_id=1, source_target_pairs={{0,2},{2,0},{1,3},{3,1},{4,6},{6,4},{5,7},{7,5},{8,10},{10,8},{9,1... | collective-permute-start | bytes 3145736 | tf_op jit(solution)/shard_map/ppermute | solution.py:21
  269.8 15.2 %copy-start.8 = (bf16[4,16,64,256]{3,2,1,0:T(8,128)(2,1)S(1)}, bf16[4,16,64,256]{3,2,1,0:T(8,128)(2,1)}, u32[]{:S(2)}) copy-start(bf16[4,16,64,256]{3,2,1,0:T(8,128)(2,1)} %get-tuple-element.24.keep_ref) | copy-start | bytes 6291460
